TPU v7x, 512 devices: a whole 4x4x16 slice. The times are simulated.
512 devices in a mesh: band: 16 (over y, z_lo), fft: 32 (over z_hi, x, core).
Axes of the slice: x: 4, y: 4, z: 16 (z_hi: 4, z_lo: 4; z = z_hi * 4 + z_lo), core: 2. Of those that a mesh axis runs over, the one named last changes fastest.
Arguments:
- orbitals: float32 [64, 128, 128, 128], P('band', 'fft'), may hold values from -6 to 6
- kernel: float32 [128, 128, 128], P(None, 'fft'), as said below
- owners: int32 [2], replicated, may hold values from 0 to 15, as said below
- picks: int32 [2, 1], replicated, may hold values from 0 to 3, as said below
Outputs:
- exchange_action: float32 [64, 128, 128, 128], P('band', 'fft')
Inputs may be any that keep to these rules, and one draw needn't show every extreme that they name: kernel is positive and takes equal values at each frequency vector and at its negative, indices taken modulo 128. `owners`: the steps name different band groups. `picks`: all entries are different positions.
All inputs are finite; a program needn't handle non-finite values.
Results may differ from a plain program's by a relative error of at most 0.00016.
Values sent between devices are 32-bit elements; how exact they have to be, the bound alone decides.
No kernel may reach another device: no remote copies, remote signals or barrier semaphores. Data moves between devices by JAX's collectives and lax.ppermute only.
A program may use at most 64 MiB of HBM per device.

v0:
```python
import math

import jax
import jax.numpy as jnp
from jax import lax
from jax.sharding import PartitionSpec as P

HIGH = lax.Precision.HIGHEST


def broadcast(block, axis, owner):
    block = jnp.where(lax.axis_index(axis) == owner, block, jnp.zeros_like(block))
    return lax.psum(block, axis)


def tables(count):
    freq = jnp.arange(count, dtype=jnp.int32)
    product = freq[:, None] * freq[None, :] % count
    angle = product.astype(jnp.float32) * (2.0 * math.pi / count)
    return (jnp.cos(angle), jnp.sin(angle))


def apply_table(values, table, axis):
    if axis == 3:
        return jnp.einsum("pxyz,zk->pxyk", values, table, precision=HIGH)
    if axis == 2:
        return jnp.einsum("pxyz,yk->pxkz", values, table, precision=HIGH)
    return jnp.einsum("pxyz,xk->pkyz", values, table, precision=HIGH)


def transform(real_part, imag_part, axis, sign, pair):
    cosine, sine = pair
    if imag_part is None:
        return (apply_table(real_part, cosine, axis), sign * apply_table(real_part, sine, axis))
    out_real = apply_table(real_part, cosine, axis) - sign * apply_table(imag_part, sine, axis)
    out_imag = apply_table(imag_part, cosine, axis) + sign * apply_table(real_part, sine, axis)
    return (out_real, out_imag)


def real_only(real_part, imag_part, axis, pair):
    cosine, sine = pair
    return apply_table(real_part, cosine, axis) - apply_table(imag_part, sine, axis)


def potential(density, kernel, pair):
    count = density.shape[3]
    real_part, imag_part = transform(density, None, 3, -1.0, pair)
    real_part, imag_part = transform(real_part, imag_part, 2, -1.0, pair)
    col_real, col_imag = transform(
        lax.all_to_all(real_part, "fft", split_axis=2, concat_axis=1, tiled=True),
        lax.all_to_all(imag_part, "fft", split_axis=2, concat_axis=1, tiled=True),
        1,
        -1.0,
        pair,
    )
    col_real = col_real * kernel
    col_imag = col_imag * kernel
    col_real, col_imag = transform(col_real, col_imag, 1, 1.0, pair)
    real_part = lax.all_to_all(col_real, "fft", split_axis=1, concat_axis=2, tiled=True)
    imag_part = lax.all_to_all(col_imag, "fft", split_axis=1, concat_axis=2, tiled=True)
    real_part, imag_part = transform(real_part, imag_part, 2, 1.0, pair)
    scale = 1.0 / float(count) ** 3
    return real_only(real_part, imag_part, 3, pair) * scale


def body(orbitals, kernel, owners, picks):
    count = orbitals.shape[3]
    local_count = orbitals.shape[0]
    sent_count = picks.shape[1]
    pair = tables(count)
    total = jnp.zeros(orbitals.shape, jnp.float32)
    for step in range(owners.shape[0]):
        chosen = jnp.take(orbitals, picks[step], axis=0)
        chosen = broadcast(chosen, "band", owners[step])
        density = (orbitals[:, None] * chosen[None]).reshape(
            (local_count * sent_count,) + orbitals.shape[1:]
        )
        field = potential(density, kernel, pair)
        field = field.reshape((local_count, sent_count) + orbitals.shape[1:])
        total = total - jnp.sum(chosen[None] * field, axis=1)
    return total


def solution(mesh):
    placed = (P("band", "fft", None, None), P(None, "fft", None), P(), P())
    return jax.shard_map(
        body, mesh=mesh, in_specs=placed, out_specs=P("band", "fft", None, None), check_vma=False
    )
```

profile of v0, /device:TPU:11, one launch (start us, length us, event | category | flops | bytes accessed | tf_op | source)
XLA Modules:
  0.0 696.7 jit_solution(12416886566960991193)
XLA Ops:
  11.8 1.4 fusion.310
  14.5 1.9 fusion.43
  16.4 160.9 %all-reduce.3.cloned.1.call-done = (f32[4,128,128]{2,1,0:T(8,128)}, f32[4,128,128]{2,1,0:T(8,128)}) async-done(((f32[4,128,128]{2,1,0:T(8,128)}, f32[4,128,128]{2,1,0:T(8,128)}), (f32[4,128,128]{2,1,0:T(8,128)}, f32[4,128,128]{2,1,0:T(8,128)})) %all-reduce.3.cloned.1.call-update) | async-done | bytes 524304 | tf_op jit(solution)/shard_map/psum | solution.py:13
  177.3 2.2 fusion.33
  180.8 1.3 fusion.75
  182.1 1.3 fusion.10
  183.4 1.6 copy.94
  185.1 25.0 %all-to-all-start.4 = ((f32[4,4,128,128]{3,1,0,2:T(4,128)}), f32[4,4,128,128]{3,1,0,2:T(4,128)}, u32[]{:S(2)}, u32[]{:S(2)}) async-start(f32[4,4,128,128]{3,1,0,2:T(4,128)} %copy.94), calls=%async_computation.4 | async-start | bytes 2097152 | tf_op jit(solution)/shard_map/all_to_all | solution.py:50
  211.3 1.3 fusion.8
  212.6 1.6 copy.99
  214.3 47.2 %all-to-all-done.4 = f32[4,4,128,128]{3,1,0,2:T(4,128)} async-done(((f32[4,4,128,128]{3,1,0,2:T(4,128)}), f32[4,4,128,128]{3,1,0,2:T(4,128)}, u32[]{:S(2)}, u32[]{:S(2)}) %all-to-all-start.4) | async-done | bytes 1048608 | tf_op jit(solution)/shard_map/all_to_all | solution.py:50
  261.5 9.7 %all-to-all-start.5 = ((f32[4,4,128,128]{3,1,0,2:T(4,128)}), f32[4,4,128,128]{3,1,0,2:T(4,128)}, u32[]{:S(2)}, u32[]{:S(2)}) async-start(f32[4,4,128,128]{3,1,0,2:T(4,128)} %copy.99), calls=%async_computation.5 | async-start | bytes 2097152 | tf_op jit(solution)/shard_map/all_to_all | solution.py:51
  272.5 1.3 fusion.97
  275.0 1.3 fusion.21
  276.3 1.6 copy.69
  278.0 43.9 %all-to-all-done.5 = f32[4,4,128,128]{3,1,0,2:T(4,128)} async-done(((f32[4,4,128,128]{3,1,0,2:T(4,128)}), f32[4,4,128,128]{3,1,0,2:T(4,128)}, u32[]{:S(2)}, u32[]{:S(2)}) %all-to-all-start.5) | async-done | bytes 1048608 | tf_op jit(solution)/shard_map/all_to_all | solution.py:51
  321.8 9.2 %all-to-all-start = ((f32[4,4,128,128]{3,1,0,2:T(4,128)}), f32[4,4,128,128]{3,1,0,2:T(4,128)S(1)}, u32[]{:S(2)}, u32[]{:S(2)}) async-start(f32[4,4,128,128]{3,1,0,2:T(4,128)} %copy.69), calls=%async_computation | async-start | bytes 2097152 | tf_op jit(solution)/shard_map/all_to_all | solution.py:50
  331.0 1.3 fusion.89
  332.3 1.3 fusion.19
  333.6 1.6 copy.74
  335.3 46.4 %all-to-all-done = f32[4,4,128,128]{3,1,0,2:T(4,128)S(1)} async-done(((f32[4,4,128,128]{3,1,0,2:T(4,128)}), f32[4,4,128,128]{3,1,0,2:T(4,128)S(1)}, u32[]{:S(2)}, u32[]{:S(2)}) %all-to-all-start) | async-done | bytes 1048608 | tf_op jit(solution)/shard_map/all_to_all | solution.py:50
  382.7 9.7 %all-to-all-start.1 = ((f32[4,4,128,128]{3,1,0,2:T(4,128)}), f32[4,4,128,128]{3,1,0,2:T(4,128)S(1)}, u32[]{:S(2)}, u32[]{:S(2)}) async-start(f32[4,4,128,128]{3,1,0,2:T(4,128)} %copy.74), calls=%async_computation.1 | async-start | bytes 2097152 | tf_op jit(solution)/shard_map/all_to_all | solution.py:51
  392.4 1.5 copy.95
  393.9 1.5 copy.100
  395.4 1.3 fusion.77
  396.7 1.3 fusion.71
  397.9 1.3 fusion.29
  400.6 1.3 fusion.31
  401.9 1.3 fusion.4
  403.2 1.6 copy.106
  404.9 33.6 %all-to-all-done.1 = f32[4,4,128,128]{3,1,0,2:T(4,128)S(1)} async-done(((f32[4,4,128,128]{3,1,0,2:T(4,128)}), f32[4,4,128,128]{3,1,0,2:T(4,128)S(1)}, u32[]{:S(2)}, u32[]{:S(2)}) %all-to-all-start.1) | async-done | bytes 1048608 | tf_op jit(solution)/shard_map/all_to_all | solution.py:51
  439.4 9.5 %all-to-all-start.6 = ((f32[4,128,4,128]{3,2,0,1:T(4,128)}), f32[4,128,4,128]{3,2,0,1:T(4,128)S(1)}, u32[]{:S(2)}, u32[]{:S(2)}) async-start(f32[4,128,4,128]{3,2,0,1:T(4,128)} %copy.106), calls=%async_computation.6 | async-start | bytes 2097152 | tf_op jit(solution)/shard_map/all_to_all | solution.py:59
  448.9 1.3 fusion.69
  450.2 1.3 fusion.3
  451.5 1.7 copy.111
  453.2 45.5 %all-to-all-done.6 = f32[4,128,4,128]{3,2,0,1:T(4,128)S(1)} async-done(((f32[4,128,4,128]{3,2,0,1:T(4,128)}), f32[4,128,4,128]{3,2,0,1:T(4,128)S(1)}, u32[]{:S(2)}, u32[]{:S(2)}) %all-to-all-start.6) | async-done | bytes 1048608 | tf_op jit(solution)/shard_map/all_to_all | solution.py:59
  498.7 9.3 %all-to-all-start.7 = ((f32[4,128,4,128]{3,2,0,1:T(4,128)}), f32[4,128,4,128]{3,2,0,1:T(4,128)}, u32[]{:S(2)}, u32[]{:S(2)}) async-start(f32[4,128,4,128]{3,2,0,1:T(4,128)} %copy.111), calls=%async_computation.7 | async-start | bytes 2097152 | tf_op jit(solution)/shard_map/all_to_all | solution.py:60
  509.5 1.3 fusion.99
  510.8 1.3 fusion.87
  512.1 1.3 fusion.23
  513.5 1.3 fusion.101
  514.8 1.3 fusion.25
  516.1 1.3 fusion.15
  517.4 1.6 copy.82
  519.1 34.8 %all-to-all-done.7 = f32[4,128,4,128]{3,2,0,1:T(4,128)} async-done(((f32[4,128,4,128]{3,2,0,1:T(4,128)}), f32[4,128,4,128]{3,2,0,1:T(4,128)}, u32[]{:S(2)}, u32[]{:S(2)}) %all-to-all-start.7) | async-done | bytes 1048608 | tf_op jit(solution)/shard_map/all_to_all | solution.py:60
  553.8 12.8 %all-to-all-start.2 = ((f32[4,128,4,128]{3,2,0,1:T(4,128)}), f32[4,128,4,128]{3,2,0,1:T(4,128)}, u32[]{:S(2)}, u32[]{:S(2)}) async-start(f32[4,128,4,128]{3,2,0,1:T(4,128)} %copy.82), calls=%async_computation.2 | async-start | bytes 2097152 | tf_op jit(solution)/shard_map/all_to_all | solution.py:59
  566.7 1.3 fusion.85
  568.0 1.3 fusion.14
  569.3 1.6 copy.87
  570.9 46.8 %all-to-all-done.2 = f32[4,128,4,128]{3,2,0,1:T(4,128)} async-done(((f32[4,128,4,128]{3,2,0,1:T(4,128)}), f32[4,128,4,128]{3,2,0,1:T(4,128)}, u32[]{:S(2)}, u32[]{:S(2)}) %all-to-all-start.2) | async-done | bytes 1048608 | tf_op jit(solution)/shard_map/all_to_all | solution.py:59
  617.8 9.4 %all-to-all-start.3 = ((f32[4,128,4,128]{3,2,0,1:T(4,128)}), f32[4,128,4,128]{3,2,0,1:T(4,128)}, u32[]{:S(2)}, u32[]{:S(2)}) async-start(f32[4,128,4,128]{3,2,0,1:T(4,128)} %copy.87), calls=%async_computation.3 | async-start | bytes 2097152 | tf_op jit(solution)/shard_map/all_to_all | solution.py:60
  628.3 1.5 copy.112
  629.8 1.5 copy.83
  631.3 1.3 fusion.81
  632.6 1.3 fusion.67
  633.9 1.3 fusion.2
  635.2 2.2 fusion.91
  638.7 1.3 fusion.1
  640.0 39.1 %all-to-all-done.3 = f32[4,128,4,128]{3,2,0,1:T(4,128)} async-done(((f32[4,128,4,128]{3,2,0,1:T(4,128)}), f32[4,128,4,128]{3,2,0,1:T(4,128)}, u32[]{:S(2)}, u32[]{:S(2)}) %all-to-all-start.3) | async-done | bytes 1048608 | tf_op jit(solution)/shard_map/all_to_all | solution.py:60
  679.0 1.5 copy.88
  680.5 1.3 fusion.83
  681.8 1.3 fusion.13
  684.4 1.5 fusion.12
  687.2 2.2 fusion.27
  (44 shorter events, 15.8 us)
Async XLA Ops:
  6.5 0.7 copy-start.13
  6.5 170.8 %copy-start = (f32[4,4,128,128]{3,2,1,0:T(8,128)S(1)}, f32[4,4,128,128]{3,2,1,0:T(8,128)}, u32[]{:S(2)}) copy-start(f32[4,4,128,128]{3,2,1,0:T(8,128)} %param.6) | copy-start | bytes 3145732
  6.5 170.8 %all-reduce.3.cloned.1.call-start = ((), (), s32[]{:S(2)}) async-start(), calls=%async_computation.8 | async-start | bytes 1048576 | tf_op jit(solution)/shard_map/psum | solution.py:13
  177.3 2.2 copy-start.6
  185.1 76.4 %all-to-all-start.4 = ((f32[4,4,128,128]{3,1,0,2:T(4,128)}), f32[4,4,128,128]{3,1,0,2:T(4,128)}, u32[]{:S(2)}, u32[]{:S(2)}) async-start(f32[4,4,128,128]{3,1,0,2:T(4,128)} %copy.94), calls=%async_computation.4 | async-start | bytes 2097152 | tf_op jit(solution)/shard_map/all_to_all | solution.py:50
  214.3 57.0 %copy-start.8 = (f32[4,128,128]{2,1,0:T(8,128)S(1)}, f32[4,128,128]{2,1,0:T(8,128)}, u32[]{:S(2)}) copy-start(f32[4,128,128]{2,1,0:T(8,128)} %get-tuple-element.18) | copy-start | bytes 786436
  261.5 60.3 %all-to-all-start.5 = ((f32[4,4,128,128]{3,1,0,2:T(4,128)}), f32[4,4,128,128]{3,1,0,2:T(4,128)}, u32[]{:S(2)}, u32[]{:S(2)}) async-start(f32[4,4,128,128]{3,1,0,2:T(4,128)} %copy.99), calls=%async_computation.5 | async-start | bytes 2097152 | tf_op jit(solution)/shard_map/all_to_all | solution.py:51
  321.8 59.9 %all-to-all-start = ((f32[4,4,128,128]{3,1,0,2:T(4,128)}), f32[4,4,128,128]{3,1,0,2:T(4,128)S(1)}, u32[]{:S(2)}, u32[]{:S(2)}) async-start(f32[4,4,128,128]{3,1,0,2:T(4,128)} %copy.69), calls=%async_computation | async-start | bytes 2097152 | tf_op jit(solution)/shard_map/all_to_all | solution.py:50
  335.3 57.1 %copy-start.12 = (f32[128,4,128]{2,1,0:T(4,128)S(1)}, f32[128,4,128]{2,1,0:T(4,128)}, u32[]{:S(2)}) copy-start(f32[128,4,128]{2,1,0:T(4,128)} %param.7) | copy-start | bytes 786436
  381.7 1.0 copy-start.1
  382.7 55.8 %all-to-all-start.1 = ((f32[4,4,128,128]{3,1,0,2:T(4,128)}), f32[4,4,128,128]{3,1,0,2:T(4,128)S(1)}, u32[]{:S(2)}, u32[]{:S(2)}) async-start(f32[4,4,128,128]{3,1,0,2:T(4,128)} %copy.74), calls=%async_computation.1 | async-start | bytes 2097152 | tf_op jit(solution)/shard_map/all_to_all | solution.py:51
  438.4 1.0 copy-start.3
  439.4 59.3 %all-to-all-start.6 = ((f32[4,128,4,128]{3,2,0,1:T(4,128)}), f32[4,128,4,128]{3,2,0,1:T(4,128)S(1)}, u32[]{:S(2)}, u32[]{:S(2)}) async-start(f32[4,128,4,128]{3,2,0,1:T(4,128)} %copy.106), calls=%async_computation.6 | async-start | bytes 2097152 | tf_op jit(solution)/shard_map/all_to_all | solution.py:59
  453.2 54.8 %copy-start.2 = (f32[4,4,128,128]{3,1,0,2:T(4,128)S(1)}, f32[4,4,128,128]{3,1,0,2:T(4,128)}, u32[]{:S(2)}) copy-start(f32[4,4,128,128]{3,1,0,2:T(4,128)} %copy-done.1) | copy-start | bytes 3145732
  498.7 55.1 %all-to-all-start.7 = ((f32[4,128,4,128]{3,2,0,1:T(4,128)}), f32[4,128,4,128]{3,2,0,1:T(4,128)}, u32[]{:S(2)}, u32[]{:S(2)}) async-start(f32[4,128,4,128]{3,2,0,1:T(4,128)} %copy.111), calls=%async_computation.7 | async-start | bytes 2097152 | tf_op jit(solution)/shard_map/all_to_all | solution.py:60
  508.0 1.2 copy-start.4
  553.8 63.9 %all-to-all-start.2 = ((f32[4,128,4,128]{3,2,0,1:T(4,128)}), f32[4,128,4,128]{3,2,0,1:T(4,128)}, u32[]{:S(2)}, u32[]{:S(2)}) async-start(f32[4,128,4,128]{3,2,0,1:T(4,128)} %copy.82), calls=%async_computation.2 | async-start | bytes 2097152 | tf_op jit(solution)/shard_map/all_to_all | solution.py:59
  570.9 56.2 %copy-start.7 = (f32[4,128,128]{2,1,0:T(8,128)S(1)}, f32[4,128,128]{2,1,0:T(8,128)}, u32[]{:S(2)}) copy-start(f32[4,128,128]{2,1,0:T(8,128)} %get-tuple-element.17) | copy-start | bytes 786436
  570.9 56.3 %copy-start.9 = (f32[4,128,128]{2,1,0:T(8,128)S(1)}, f32[4,128,128]{2,1,0:T(8,128)}, u32[]{:S(2)}) copy-start(f32[4,128,128]{2,1,0:T(8,128)} %get-tuple-element.18) | copy-start | bytes 786436
  617.8 61.3 %all-to-all-start.3 = ((f32[4,128,4,128]{3,2,0,1:T(4,128)}), f32[4,128,4,128]{3,2,0,1:T(4,128)}, u32[]{:S(2)}, u32[]{:S(2)}) async-start(f32[4,128,4,128]{3,2,0,1:T(4,128)} %copy.87), calls=%async_computation.3 | async-start | bytes 2097152 | tf_op jit(solution)/shard_map/all_to_all | solution.py:60
  684.4 1.6 copy-start.5
  684.4 1.6 copy-start.11
  686.0 1.2 copy-start.10
Sparse Core Ops, SparseCore 0:
  16.5 160.7 all-reduce.2
where the time goes:
time: 706 us; the launch traced here: 697 us
  waiting for transfers between devices  498 us (71%)
  starting transfers between devices  94.6 us (13%)
  matrix products  54.5 us (8%)
  local copies, waits for them, and re-layouts  27 us (4%)
  between operations  19.7 us (3%)
    psum x1, waiting for transfers between devices, broadcast(): return lax.psum(block, axis)  161 us
    all_to_all x2, waiting for transfers between devices, potential(): lax.all_to_all(real_part, 'fft', split_axis=2, concat_axis=1, tiled=True)  93.7 us
    all_to_all x2, waiting for transfers between devices, potential(): lax.all_to_all(col_real, 'fft', split_axis=1, concat_axis=2, tiled=True)  92.4 us
    all_to_all x2, waiting for transfers between devices, potential(): lax.all_to_all(imag_part, 'fft', split_axis=2, concat_axis=1, tiled=True)  77.4 us
    all_to_all x2, waiting for transfers between devices, potential(): lax.all_to_all(col_imag, 'fft', split_axis=1, concat_axis=2, tiled=True)  73.8 us
    all_to_all x2, starting transfers between devices, potential(): lax.all_to_all(real_part, 'fft', split_axis=2, concat_axis=1, tiled=True)  34.1 us
    all_to_all x2, starting transfers between devices, potential(): lax.all_to_all(col_real, 'fft', split_axis=1, concat_axis=2, tiled=True)  22.3 us
    dot_general x16, matrix products, apply_table(): return jnp.einsum('pxyz,yk->pxkz', values, table, precision=HIGH)  20.9 us
  transfers between devices with their start and end apart: 9, of which 9 were waited for; matrix products, arithmetic and copies ran while one was open for 8% of the time, Pallas kernels for 0%

commit v1 on v0

v1 whole, which is shorter than its diff:
```python
import functools

import jax
import jax.numpy as jnp
import ml_dtypes
import numpy as np
from jax import lax
from jax.experimental import pallas as pl
from jax.experimental.pallas import tpu as pltpu
from jax.sharding import Mesh, PartitionSpec as P

NG = 128
SIDE = 4
GROUP = 32
SCALE = 1.0 / float(NG) ** 3


def split_table(matrix):
    high = matrix.astype(np.float32).astype(ml_dtypes.bfloat16)
    low = (matrix - high.astype(np.float64)).astype(ml_dtypes.bfloat16)
    return np.stack([high, low])


def real_form(rows, cols, sign):
    angle = 2.0 * np.pi * ((rows[:, None] * cols[None, :]) % NG) / NG
    cosine, sine = np.cos(angle), sign * np.sin(angle)
    return np.block([[cosine, -sine], [sine, cosine]])


def make_tables():
    plain = np.arange(NG)
    rank = np.arange(GROUP)
    y, x, core = rank // 8, rank // 2 % 4, rank % 2
    held = (np.arange(SIDE)[None, :] * 32 + (x * 8 + core * 4 + y)[:, None]).reshape(-1)
    mixed = (rank[:, None, None] * SIDE + np.arange(2)[None, :, None] * NG + np.arange(SIDE)[None, None, :]).reshape(-1)
    z_fwd = real_form(plain, plain, -1.0).T
    y_fwd = real_form(held, plain, -1.0)[mixed]
    x_fwd = real_form(plain, held, -1.0)
    x_inv = real_form(held, plain, 1.0)
    y_inv = real_form(plain, held, 1.0)[:, mixed]
    z_inv = real_form(plain, plain, 1.0).T
    return [split_table(t) for t in (z_fwd, y_fwd, x_fwd, x_inv, y_inv, z_inv)]


def split(values):
    high = values.astype(jnp.bfloat16)
    return high, (values - high.astype(jnp.float32)).astype(jnp.bfloat16)


def dot(a, b):
    return jnp.dot(a, b, preferred_element_type=jnp.float32)


def times(values, table):
    high, low = split(values)
    return dot(high, table[0]) + (dot(low, table[0]) + dot(high, table[1]))


def apply(table, values):
    high, low = split(values)
    return dot(table[0], high) + (dot(table[0], low) + dot(table[1], high))


def forward_kernel(psi_ref, sent_ref, z_ref, y_ref, out_ref):
    def per_plane(b, carry):
        base = pl.multiple_of(b * SIDE, SIDE)
        first = sent_ref[pl.ds(base, SIDE), 0].reshape(NG, NG)
        second = sent_ref[pl.ds(base, SIDE), 1].reshape(NG, NG)
        rows = []
        for a in range(SIDE):
            psi = psi_ref[base + a]
            rows.append(jnp.concatenate([psi * first, psi * second], axis=1))
        lines = times(jnp.concatenate(rows, axis=0), z_ref)
        cols = []
        for a in range(SIDE):
            part = lines[a * NG : (a + 1) * NG]
            cols.append(jnp.concatenate([part[:, :NG], part[:, NG:]], axis=0))
        spectrum = apply(y_ref, jnp.concatenate(cols, axis=1))
        for a in range(SIDE):
            out_ref[:, base + a] = spectrum[:, a * NG : (a + 1) * NG].reshape(GROUP, 8, NG)
        return carry

    lax.fori_loop(0, SIDE, per_plane, 0)


def middle_kernel(in_ref, kernel_ref, fwd_ref, inv_ref, out_ref):
    for ky in range(SIDE):
        cols = []
        for a in range(SIDE):
            at = a * 8 + ky
            cols.append(
                jnp.concatenate([in_ref[pl.ds(at, NG, stride=32), :], in_ref[pl.ds(at + 4, NG, stride=32), :]], axis=0)
            )
        spectrum = apply(fwd_ref, jnp.concatenate(cols, axis=1))
        weight = kernel_ref[ky]
        weight = jnp.concatenate([weight, weight], axis=0)
        weight = jnp.concatenate([weight] * SIDE, axis=1)
        back = apply(inv_ref, spectrum * weight)
        for a in range(SIDE):
            at = a * 8 + ky
            part = back[:, a * NG : (a + 1) * NG]
            out_ref[pl.ds(at, NG, stride=32), :] = part[:NG]
            out_ref[pl.ds(at + 4, NG, stride=32), :] = part[NG:]


def inverse_kernel(in_ref, sent_ref, y_ref, z_ref, out_ref):
    def per_plane(b, carry):
        base = pl.multiple_of(b * SIDE, SIDE)
        first = sent_ref[pl.ds(base, SIDE), 0].reshape(NG, NG)
        second = sent_ref[pl.ds(base, SIDE), 1].reshape(NG, NG)
        cols = [in_ref[:, base + a].reshape(2 * NG, NG) for a in range(SIDE)]
        lines = apply(y_ref, jnp.concatenate(cols, axis=1))
        rows = []
        for a in range(SIDE):
            part = lines[:, a * NG : (a + 1) * NG]
            rows.append(jnp.concatenate([part[:NG], part[NG:]], axis=1))
        field = times(jnp.concatenate(rows, axis=0), z_ref)
        for a in range(SIDE):
            part = field[a * NG : (a + 1) * NG]
            out_ref[base + a] = (first * part[:, :NG] + second * part[:, NG:]) * (-SCALE)
        return carry

    lax.fori_loop(0, SIDE, per_plane, 0)


def call(kernel, shape, flops, *args):
    moved = sum(int(np.prod(a.shape)) * a.dtype.itemsize for a in args) + 4 * int(np.prod(shape))
    return pl.pallas_call(
        kernel,
        out_shape=jax.ShapeDtypeStruct(shape, jnp.float32),
        compiler_params=pltpu.CompilerParams(vmem_limit_bytes=40 * 1024 * 1024),
        cost_estimate=pl.CostEstimate(flops=flops, bytes_accessed=moved, transcendentals=0),
    )(*args)


def body(tables, orbitals, kernel, owners, picks):
    z_fwd, y_fwd, x_fwd, x_inv, y_inv, z_inv = [jnp.asarray(t) for t in tables]
    steps = owners.shape[0]

    chosen = jnp.take(orbitals, picks[:, 0], axis=0).reshape(steps, SIDE, SIDE, 32, NG)
    chosen = jnp.transpose(chosen, (1, 2, 0, 3, 4)).reshape(SIDE * SIDE, steps, 32, NG)
    offered = lax.all_to_all(chosen, ("y", "zl"), 0, 0, tiled=True)
    piece = jnp.stack([lax.dynamic_index_in_dim(offered, owners[s], 0, keepdims=False)[s] for s in range(steps)])

    orbitals, piece = lax.optimization_barrier((orbitals.reshape(SIDE * SIDE, NG, NG), piece))
    sent = lax.all_gather(piece, ("zh", "zl"), axis=0, tiled=False)
    psi = lax.all_to_all(orbitals, ("zh", "y"), 0, 0, tiled=True)

    own = lax.dynamic_index_in_dim(kernel, lax.axis_index("y"), 1, keepdims=False)
    own, psi = lax.optimization_barrier((own, psi))
    weight = lax.all_gather(own, "zh", axis=0, tiled=False)

    work = 2 * 2 * 3 * 2048 * 256 * 256
    group = ("y", "x", "c")
    spectrum = call(forward_kernel, (GROUP, 16, 8, NG), work, psi, sent, z_fwd, y_fwd)
    spectrum = lax.all_to_all(spectrum, group, 0, 0, tiled=True).reshape(GROUP * NG, NG)
    spectrum = call(middle_kernel, (GROUP * NG, NG), work, spectrum, weight, x_fwd, x_inv)
    spectrum = lax.all_to_all(spectrum.reshape(GROUP, 16, 8, NG), group, 0, 0, tiled=True)
    action = call(inverse_kernel, (16, NG, NG), work, spectrum, sent, y_inv, z_inv)
    action = lax.all_to_all(action, ("zh", "y"), 0, 0, tiled=True)
    return action.reshape(SIDE, SIDE, NG, NG)


def solution(mesh):
    fine = Mesh(np.asarray(mesh.devices).reshape(4, 4, 4, 4, 2), ("y", "zl", "zh", "x", "c"))
    band, fft = ("y", "zl"), ("zh", "x", "c")
    placed = (P(band, fft, None, None), P(None, fft, None), P(), P())
    return jax.shard_map(
        functools.partial(body, make_tables()),
        mesh=fine,
        in_specs=placed,
        out_specs=P(band, fft, None, None),
        check_vma=False,
    )
```

time: 706 us -> 263 us (0.37)
  the two profiles are of different devices: /device:TPU:11 before, /device:TPU:24 now
where the time goes in v1:
time: 263 us; the launch traced here: 262 us
  blocking collectives  191 us (73%)
  starting transfers between devices  31.9 us (12%)
  waiting for transfers between devices  16.2 us (6%)
  Pallas kernels  11.4 us (4%)
  local copies, waits for them, and re-layouts  5.7 us (2%)
  between operations  3.64 us (1%)
    all_gather x1, blocking collectives, body(): sent = lax.all_gather(piece, ('zh', 'zl'), axis=0, tiled=False)  73.4 us
    all_to_all x1, blocking collectives, body(): action = lax.all_to_all(action, ('zh', 'y'), 0, 0, tiled=True)  64.5 us
    all_to_all x1, blocking collectives, body(): lax.all_to_all(spectrum.reshape(GROUP, 16, 8, NG), group, 0, 0, tiled=True)  32.3 us
    all_gather x1, blocking collectives, body(): weight = lax.all_gather(own, 'zh', axis=0, tiled=False)  20.9 us
    all_to_all x1, starting transfers between devices, body(): psi = lax.all_to_all(orbitals, ('zh', 'y'), 0, 0, tiled=True)  15.1 us
    pallas_call x3, Pallas kernels, call(): pl.pallas_call(kernel, out_shape=jax.ShapeDtypeStruct(shape, jnp.float32)...  11.4 us
    all_to_all x1, waiting for transfers between devices, body(): offered = lax.all_to_all(chosen, ('y', 'zl'), 0, 0, tiled=True)  9.85 us
    all_to_all x1, starting transfers between devices, body(): offered = lax.all_to_all(chosen, ('y', 'zl'), 0, 0, tiled=True)  9.16 us
  transfers between devices with their start and end apart: 3, of which 2 were waited for; matrix products, arithmetic and copies ran while one was open for 0% of the time, Pallas kernels for 0%

profile of v1, /device:TPU:24, one launch (start us, length us, event | category | flops | bytes accessed | tf_op | source)
XLA Modules:
  0.0 262.2 jit_solution(10414210701216309920)
XLA Ops:
  0.0 0.0 copy-start
  0.0 0.0 copy-start.8
  0.0 0.7 fusion
  0.7 0.7 and_bitcast_fusion
  1.4 1.8 gather_fusion
  3.2 0.9 copy_select_fusion
  4.1 0.0 copy-start.6
  4.1 0.0 copy-start.7
  4.1 9.2 %all-to-all-start = ((f32[16,2,32,128]{3,2,1,0:T(8,128)}), f32[16,2,32,128]{3,2,1,0:T(8,128)S(1)}, u32[]{:S(2)}, u32[]{:S(2)}) async-start(f32[16,2,32,128]{3,2,1,0:T(8,128)} %bitcast.6), calls=%async_computation | async-start | bytes 1048576 | tf_op jit(solution)/shard_map/all_to_all | solution.py:142
  13.3 0.0 copy-done.8
  13.3 0.6 fusion.1
  17.4 9.8 %all-to-all-done = f32[16,2,32,128]{3,2,1,0:T(8,128)S(1)} async-done(((f32[16,2,32,128]{3,2,1,0:T(8,128)}), f32[16,2,32,128]{3,2,1,0:T(8,128)S(1)}, u32[]{:S(2)}, u32[]{:S(2)}) %all-to-all-start) | async-done | bytes 524320 | tf_op jit(solution)/shard_map/all_to_all | solution.py:142
  27.3 15.1 %all-to-all-start.1 = ((f32[16,128,128]{2,1,0:T(8,128)}), f32[16,128,128]{2,1,0:T(8,128)S(1)}, u32[]{:S(2)}, u32[]{:S(2)}) async-start(f32[16,128,128]{2,1,0:T(8,128)} %bitcast.1), calls=%async_computation.1 | async-start | bytes 2097152 | tf_op jit(solution)/shard_map/all_to_all | solution.py:147
  42.4 0.0 copy-done
  42.4 0.1 constant_dynamic-slice_fusion
  42.4 73.4 %all-gather = f32[32,32,128]{2,1,0:T(8,128)S(1)} all-gather(f32[2,32,128]{2,1,0:T(8,128)S(1)} %pad_maximum_fusion), channel_id=2, replica_groups=mesh['y'=4,'zl'=4,'zh'=4,'x'=4,'c'=2] {'zh','zl'}, dimensions={0}, use_global_device_ids=true | all-gather | bytes 557056 | tf_op jit(solution)/shard_map/all_gather | solution.py:146
  115.8 0.0 all-to-all-done.1.psi_ref
  115.8 0.0 copy-done.6
  115.8 0.0 copy-done.7
  115.8 4.1 %shard_map.100 = f32[32,16,8,128]{3,2,1,0:T(8,128)S(1)} custom-call(f32[16,128,128]{2,1,0:T(8,128)S(1)} %all-to-all-done.1.psi_ref, f32[16,2,32,128]{3,2,1,0:T(8,128)S(1)} %bitcast.23, bf16[2,256,256]{2,1,0:T(8,128)(2,1)S(1)} %copy-done.6, bf16[2,256,256]{2,1,0:T(8,128)(2,1)S(1)} %copy-done.7), custom_call_target="tpu_custom_call" | custom-call | flops 1610612736 | bytes 4194304 | tf_op jit(solution)/shard_map/pallas_call | solution.py:128
  120.0 0.0 copy-start.1
  120.0 1.3 copy-done.1
  121.3 0.0 copy-start.4
  121.3 7.6 %all-to-all-start.2 = ((f32[32,16,8,128]{3,2,1,0:T(8,128)}), f32[32,16,8,128]{3,2,1,0:T(8,128)S(1)}, u32[]{:S(2)}, u32[]{:S(2)}) async-start(f32[32,16,8,128]{3,2,1,0:T(8,128)} %copy-done.1), calls=%async_computation.2 | async-start | bytes 4194304 | tf_op jit(solution)/shard_map/all_to_all | solution.py:156
  128.9 20.9 %all-gather.1 = f32[512,128]{1,0:T(8,128)S(1)} all-gather(f32[128,128]{1,0:T(8,128)S(1)} %bitcast.28), channel_id=3, replica_groups=mesh['y'=4,'zl'=4,'zh'=4,'x'=4,'c'=2] {'zh'}, dimensions={0}, use_global_device_ids=true | all-gather | bytes 327680 | tf_op jit(solution)/shard_map/all_gather | solution.py:151
  149.8 6.4 %all-to-all-done.2 = f32[32,16,8,128]{3,2,1,0:T(8,128)S(1)} async-done(((f32[32,16,8,128]{3,2,1,0:T(8,128)}), f32[32,16,8,128]{3,2,1,0:T(8,128)S(1)}, u32[]{:S(2)}, u32[]{:S(2)}) %all-to-all-start.2) | async-done | bytes 2097184 | tf_op jit(solution)/shard_map/all_to_all | solution.py:156
  156.1 0.0 copy-done.4
  156.1 0.0 copy-start.5
  156.1 0.9 copy-done.5
  157.1 4.3 %shard_map.101 = f32[4096,128]{1,0:T(8,128)S(1)} custom-call(f32[4096,128]{1,0:T(8,128)S(1)} %bitcast.21, f32[4,128,128]{2,1,0:T(8,128)S(1)} %bitcast.25, bf16[2,256,256]{2,1,0:T(8,128)(2,1)S(1)} %copy-done.4, bf16[2,256,256]{2,1,0:T(8,128)(2,1)S(1)} %copy-done.5), custom_call_target="tpu_custom_call" | custom-call | flops 1610612736 | bytes 4980736 | tf_op jit(solution)/shard_map/pallas_call | solution.py:128
  161.3 0.0 copy-start.2
  161.4 0.0 copy-start.3
  161.4 32.3 %all_to_all.25.in_ref = f32[32,16,8,128]{3,2,1,0:T(8,128)S(1)} all-to-all(f32[32,16,8,128]{3,2,1,0:T(8,128)S(1)} %bitcast.22), channel_id=1, replica_groups=mesh['y'=4,'zl'=4,'zh'=4,'x'=4,'c'=2] {'y','x','c'}, dimensions={0} | all-to-all | bytes 4194304 | tf_op jit(solution)/shard_map/all_to_all | solution.py:158
  193.7 0.0 copy-done.2
  193.7 0.0 copy-done.3
  193.7 3.0 %shard_map.102 = f32[16,128,128]{2,1,0:T(8,128)S(1)} custom-call(f32[32,16,8,128]{3,2,1,0:T(8,128)S(1)} %all_to_all.25.in_ref, f32[16,2,32,128]{3,2,1,0:T(8,128)S(1)} %bitcast.24, bf16[2,256,256]{2,1,0:T(8,128)(2,1)S(1)} %copy-done.2, bf16[2,256,256]{2,1,0:T(8,128)(2,1)S(1)} %copy-done.3), custom_call_target="tpu_custom_call" | custom-call | flops 1610612736 | bytes 4194304 | tf_op jit(solution)/shard_map/pallas_call | solution.py:128
  196.7 64.5 %all_to_all.26 = f32[16,128,128]{2,1,0:T(8,128)S(1)} all-to-all(f32[16,128,128]{2,1,0:T(8,128)S(1)} %shard_map.102), channel_id=1, replica_groups=mesh['y'=4,'zl'=4,'zh'=4,'x'=4,'c'=2] {'zh','y'}, dimensions={0} | all-to-all | bytes 2097152 | tf_op jit(solution)/shard_map/all_to_all | solution.py:160
  261.2 1.0 copy.15
  (3 shorter events, 0.0 us)
Async XLA Ops:
  0.0 42.4 %copy-start = (f32[128,4,128]{2,1,0:T(4,128)S(1)}, f32[128,4,128]{2,1,0:T(4,128)}, u32[]{:S(2)}) copy-start(f32[128,4,128]{2,1,0:T(4,128)} %param.11) | copy-start | bytes 786436
  0.0 13.3 %copy-start.8 = (s32[2]{0:T(128)S(1)}, s32[2]{0:T(128)}, u32[]{:S(2)}) copy-start(s32[2]{0:T(128)} %param.12) | copy-start | bytes 28
  4.1 111.7 %copy-start.6 = (bf16[2,256,256]{2,1,0:T(8,128)(2,1)S(1)}, bf16[2,256,256]{2,1,0:T(8,128)(2,1)}, u32[]{:S(2)}) copy-start(bf16[2,256,256]{2,1,0:T(8,128)(2,1)} %constant.45.clone.z_ref) | copy-start | bytes 786436
  4.1 111.7 %copy-start.7 = (bf16[2,256,256]{2,1,0:T(8,128)(2,1)S(1)}, bf16[2,256,256]{2,1,0:T(8,128)(2,1)}, u32[]{:S(2)}) copy-start(bf16[2,256,256]{2,1,0:T(8,128)(2,1)} %constant.46.clone.y_ref) | copy-start | bytes 786436
  4.1 23.1 %all-to-all-start = ((f32[16,2,32,128]{3,2,1,0:T(8,128)}), f32[16,2,32,128]{3,2,1,0:T(8,128)S(1)}, u32[]{:S(2)}, u32[]{:S(2)}) async-start(f32[16,2,32,128]{3,2,1,0:T(8,128)} %bitcast.6), calls=%async_computation | async-start | bytes 1048576 | tf_op jit(solution)/shard_map/all_to_all | solution.py:142
  27.3 88.6 %all-to-all-start.1 = ((f32[16,128,128]{2,1,0:T(8,128)}), f32[16,128,128]{2,1,0:T(8,128)S(1)}, u32[]{:S(2)}, u32[]{:S(2)}) async-start(f32[16,128,128]{2,1,0:T(8,128)} %bitcast.1), calls=%async_computation.1 | async-start | bytes 2097152 | tf_op jit(solution)/shard_map/all_to_all | solution.py:147
  120.0 1.3 copy-start.1
  121.3 34.8 %copy-start.4 = (bf16[2,256,256]{2,1,0:T(8,128)(2,1)S(1)}, bf16[2,256,256]{2,1,0:T(8,128)(2,1)}, u32[]{:S(2)}) copy-start(bf16[2,256,256]{2,1,0:T(8,128)(2,1)} %constant.47.clone.fwd_ref) | copy-start | bytes 786436
  121.3 34.8 %all-to-all-start.2 = ((f32[32,16,8,128]{3,2,1,0:T(8,128)}), f32[32,16,8,128]{3,2,1,0:T(8,128)S(1)}, u32[]{:S(2)}, u32[]{:S(2)}) async-start(f32[32,16,8,128]{3,2,1,0:T(8,128)} %copy-done.1), calls=%async_computation.2 | async-start | bytes 4194304 | tf_op jit(solution)/shard_map/all_to_all | solution.py:156
  156.1 1.0 copy-start.5
  161.3 32.3 %copy-start.2 = (bf16[2,256,256]{2,1,0:T(8,128)(2,1)S(1)}, bf16[2,256,256]{2,1,0:T(8,128)(2,1)}, u32[]{:S(2)}) copy-start(bf16[2,256,256]{2,1,0:T(8,128)(2,1)} %constant.49.clone.y_ref) | copy-start | bytes 786436
  161.4 32.3 %copy-start.3 = (bf16[2,256,256]{2,1,0:T(8,128)(2,1)S(1)}, bf16[2,256,256]{2,1,0:T(8,128)(2,1)}, u32[]{:S(2)}) copy-start(bf16[2,256,256]{2,1,0:T(8,128)(2,1)} %constant.50.clone.z_ref) | copy-start | bytes 786436

commit v2 on v1

v2 whole, which is shorter than its diff:
```python
import functools

import jax
import jax.numpy as jnp
import ml_dtypes
import numpy as np
from jax import lax
from jax.experimental import pallas as pl
from jax.experimental.pallas import tpu as pltpu
from jax.sharding import Mesh, PartitionSpec as P

NG = 128
SIDE = 4
GROUP = 32
SCALE = 1.0 / float(NG) ** 3


def split_table(matrix):
    high = matrix.astype(np.float32).astype(ml_dtypes.bfloat16)
    low = (matrix - high.astype(np.float64)).astype(ml_dtypes.bfloat16)
    return np.stack([high, low])


def real_form(rows, cols, sign):
    angle = 2.0 * np.pi * ((rows[:, None] * cols[None, :]) % NG) / NG
    cosine, sine = np.cos(angle), sign * np.sin(angle)
    return np.block([[cosine, -sine], [sine, cosine]])


def make_tables():
    plain = np.arange(NG)
    rank = np.arange(GROUP)
    y, x, core = rank // 8, rank // 2 % 4, rank % 2
    held = (np.arange(SIDE)[None, :] * 32 + (x * 8 + core * 4 + y)[:, None]).reshape(-1)
    mixed = (rank[:, None, None] * SIDE + np.arange(2)[None, :, None] * NG + np.arange(SIDE)[None, None, :]).reshape(-1)
    z_fwd = real_form(plain, plain, -1.0).T
    y_fwd = real_form(held, plain, -1.0)[mixed]
    x_fwd = real_form(plain, held, -1.0)
    x_inv = real_form(held, plain, 1.0)
    y_inv = real_form(plain, held, 1.0)[:, mixed]
    z_inv = real_form(plain, plain, 1.0).T
    return [split_table(t) for t in (z_fwd, y_fwd, x_fwd, x_inv, y_inv, z_inv)]


def split(values):
    high = values.astype(jnp.bfloat16)
    return high, (values - high.astype(jnp.float32)).astype(jnp.bfloat16)


def dot(a, b):
    return jnp.dot(a, b, preferred_element_type=jnp.float32)


def times(values, table):
    high, low = split(values)
    return dot(high, table[0]) + (dot(low, table[0]) + dot(high, table[1]))


def apply(table, values):
    high, low = split(values)
    return dot(table[0], high) + (dot(table[0], low) + dot(table[1], high))


def plane(sent_ref, place_ref, b, s):
    return jnp.concatenate([sent_ref[place_ref[b * SIDE + q], s] for q in range(SIDE)], axis=0)


def forward_kernel(place_ref, psi_ref, sent_ref, z_ref, y_ref, out_ref):
    for b in range(SIDE):
        first, second = plane(sent_ref, place_ref, b, 0), plane(sent_ref, place_ref, b, 1)
        rows = []
        for a in range(SIDE):
            psi = psi_ref[b * SIDE + a]
            rows.append(jnp.concatenate([psi * first, psi * second], axis=1))
        lines = times(jnp.concatenate(rows, axis=0), z_ref)
        cols = []
        for a in range(SIDE):
            part = lines[a * NG : (a + 1) * NG]
            cols.append(jnp.concatenate([part[:, :NG], part[:, NG:]], axis=0))
        spectrum = apply(y_ref, jnp.concatenate(cols, axis=1))
        for a in range(SIDE):
            out_ref[:, b * SIDE + a] = spectrum[:, a * NG : (a + 1) * NG].reshape(GROUP, 8, NG)


def middle_kernel(place_ref, in_ref, kernel_ref, fwd_ref, inv_ref, out_ref):
    for ky in range(SIDE):
        cols = []
        for a in range(SIDE):
            at = a * 8 + ky
            cols.append(
                jnp.concatenate([in_ref[pl.ds(at, NG, stride=32), :], in_ref[pl.ds(at + 4, NG, stride=32), :]], axis=0)
            )
        spectrum = apply(fwd_ref, jnp.concatenate(cols, axis=1))
        weight = kernel_ref[place_ref[16 + ky]]
        weight = jnp.concatenate([weight, weight], axis=0)
        weight = jnp.concatenate([weight] * SIDE, axis=1)
        back = apply(inv_ref, spectrum * weight)
        for a in range(SIDE):
            at = a * 8 + ky
            part = back[:, a * NG : (a + 1) * NG]
            out_ref[pl.ds(at, NG, stride=32), :] = part[:NG]
            out_ref[pl.ds(at + 4, NG, stride=32), :] = part[NG:]


def inverse_kernel(place_ref, in_ref, sent_ref, y_ref, z_ref, out_ref):
    for b in range(SIDE):
        first, second = plane(sent_ref, place_ref, b, 0), plane(sent_ref, place_ref, b, 1)
        cols = [in_ref[:, b * SIDE + a].reshape(2 * NG, NG) for a in range(SIDE)]
        lines = apply(y_ref, jnp.concatenate(cols, axis=1))
        rows = []
        for a in range(SIDE):
            part = lines[:, a * NG : (a + 1) * NG]
            rows.append(jnp.concatenate([part[:NG], part[NG:]], axis=1))
        field = times(jnp.concatenate(rows, axis=0), z_ref)
        for a in range(SIDE):
            part = field[a * NG : (a + 1) * NG]
            out_ref[b * SIDE + a] = (first * part[:, :NG] + second * part[:, NG:]) * (-SCALE)


WORK = 2 * 2 * 3 * 2048 * 256 * 256


def call(kernel, shapes, place, *args):
    moved = sum(int(np.prod(a.shape)) * a.dtype.itemsize for a in args)
    moved += 4 * sum(int(np.prod(shape)) for shape in shapes)
    shapes = [jax.ShapeDtypeStruct(shape, jnp.float32) for shape in shapes]
    whole = pl.BlockSpec(memory_space=pltpu.VMEM)
    return pl.pallas_call(
        kernel,
        out_shape=shapes,
        in_specs=[pl.BlockSpec(memory_space=pltpu.SMEM)] + [whole] * len(args),
        out_specs=[whole] * len(shapes),
        compiler_params=pltpu.CompilerParams(vmem_limit_bytes=40 * 1024 * 1024),
        cost_estimate=pl.CostEstimate(flops=WORK, bytes_accessed=moved, transcendentals=0),
    )(place, *args)


def shift(values, axes, count, by):
    return lax.ppermute(values, axes, [(i, (i + by) % count) for i in range(count)])


def body(tables, orbitals, kernel, owners, picks):
    z_fwd, y_fwd, x_fwd, x_inv, y_inv, z_inv = [jnp.asarray(t) for t in tables]
    steps = owners.shape[0]
    y, zh, zl = lax.axis_index("y"), lax.axis_index("zh"), lax.axis_index("zl")

    psi = lax.all_to_all(orbitals.reshape(SIDE * SIDE, NG, NG), ("zh", "y"), 0, 0, tiled=True)

    def select(found, distance):
        return jnp.stack([lax.select_n(distance[s], *[f[s] for f in found]) for s in range(steps)])

    found = []
    for k in range(SIDE):
        at = (y + k) % SIDE
        part = [lax.dynamic_slice(orbitals, (picks[s, 0], at, 0, 0), (1, 1, NG, NG))[0, 0] for s in range(steps)]
        found.append(jnp.stack(part) if k == 0 else shift(jnp.stack(part), "y", SIDE, k))
    chosen = select(found, (y - owners // SIDE) % SIDE).reshape(steps, SIDE, 32, NG)
    found = []
    for k in range(SIDE):
        part = lax.dynamic_index_in_dim(chosen, (zl + k) % SIDE, 1, keepdims=False)
        found.append(part if k == 0 else shift(part, "zl", SIDE, k))
    sent = select(found, (zl - owners % SIDE) % SIDE)
    sent, psi = lax.optimization_barrier((sent, psi))
    sent = lax.all_to_all(jnp.broadcast_to(sent, (SIDE,) + sent.shape), "zh", 0, 0, tiled=True)
    sent = lax.all_to_all(jnp.broadcast_to(sent, (SIDE,) + sent.shape), "zl", 0, 0, tiled=True)
    sent = sent.reshape(16, steps, 32, NG)
    place = jnp.arange(16, dtype=jnp.int32)
    quarter = place % SIDE * SIDE + place // SIDE
    place = jnp.concatenate([quarter, jnp.arange(SIDE, dtype=jnp.int32)])

    own = lax.dynamic_index_in_dim(kernel, y, 1, keepdims=False)
    own, psi, sent = lax.optimization_barrier((own, psi, sent))
    weight = lax.all_gather(own, "zh", axis=0, tiled=False)

    group = ("y", "x", "c")
    (spectrum,) = call(forward_kernel, [(GROUP, 16, 8, NG)], place, psi, sent, z_fwd, y_fwd)
    spectrum = lax.all_to_all(spectrum, group, 0, 0, tiled=True).reshape(GROUP * NG, NG)
    (spectrum,) = call(middle_kernel, [(GROUP * NG, NG)], place, spectrum, weight, x_fwd, x_inv)
    spectrum = lax.all_to_all(spectrum.reshape(GROUP, 16, 8, NG), group, 0, 0, tiled=True)
    (action,) = call(inverse_kernel, [(16, NG, NG)], place, spectrum, sent, y_inv, z_inv)
    action = lax.all_to_all(action, ("zh", "y"), 0, 0, tiled=True)
    return action.reshape(SIDE, SIDE, NG, NG)


def solution(mesh):
    fine = Mesh(np.asarray(mesh.devices).reshape(4, 4, 4, 4, 2), ("y", "zl", "zh", "x", "c"))
    band, fft = ("y", "zl"), ("zh", "x", "c")
    placed = (P(band, fft, None, None), P(None, fft, None), P(), P())
    return jax.shard_map(
        functools.partial(body, make_tables()),
        mesh=fine,
        in_specs=placed,
        out_specs=P(band, fft, None, None),
        check_vma=False,
    )
```

time: 263 us -> 250 us (0.951)
  blocking collectives: 191 us -> 134 us
  waiting for transfers between devices: 16.2 us -> 36.4 us
  starting transfers between devices: 31.9 us -> 47.7 us
  between operations: 3.64 us -> 11.8 us
    all_gather x1 -> x0, blocking collectives: 73.4 us -> none  [body(): sent = lax.all_gather(piece, ('zh', 'zl'), axis=0, tiled=False)]
    all_to_all x0 -> x1, blocking collectives: none -> 26.1 us  [body(): lax.all_to_all(jnp.broadcast_to(sent, (SIDE,) + sent.shape), 'zh', 0, 0,...]
    ppermute x0 -> x6, starting transfers between devices: none -> 18.4 us  [shift(): lax.ppermute(values, axes, [(i, (i + by) % count) for i in range(count)])]
    ppermute x0 -> x6, waiting for transfers between devices: none -> 16.2 us  [shift(): lax.ppermute(values, axes, [(i, (i + by) % count) for i in range(count)])]
    all_to_all x1, blocking collectives: 64.5 us -> 57.5 us  [body(): action = lax.all_to_all(action, ('zh', 'y'), 0, 0, tiled=True)]
    all_to_all x2, starting transfers between devices: 24.3 us -> 21.6 us  [the longest x1 18.1 us: body(): lax.all_to_all(orbitals.reshape(SIDE * SIDE, NG, NG), ('zh', 'y'), 0, 0,...]
  transfers between devices with their start and end apart: 3 -> 9, of which waited for: 2 -> 4; matrix products, arithmetic and copies ran while one was open for 0% -> 1% of each run, Pallas kernels for 0% -> 0%
where the time goes in v2:
time: 250 us; the launch traced here: 247 us
  blocking collectives  134 us (54%)
  starting transfers between devices  47.7 us (19%)
  waiting for transfers between devices  36.4 us (15%)
  between operations  11.8 us (5%)
  Pallas kernels  10.5 us (4%)
  local copies, waits for them, and re-layouts  5.52 us (2%)
    all_to_all x1, blocking collectives, body(): action = lax.all_to_all(action, ('zh', 'y'), 0, 0, tiled=True)  57.5 us
    all_to_all x1, blocking collectives, body(): lax.all_to_all(spectrum.reshape(GROUP, 16, 8, NG), group, 0, 0, tiled=True)  32.3 us
    all_to_all x1, blocking collectives, body(): lax.all_to_all(jnp.broadcast_to(sent, (SIDE,) + sent.shape), 'zh', 0, 0,...  26.1 us
    all_gather x1, blocking collectives, body(): weight = lax.all_gather(own, 'zh', axis=0, tiled=False)  18.6 us
    ppermute x6, starting transfers between devices, shift(): lax.ppermute(values, axes, [(i, (i + by) % count) for i in range(count)])  18.4 us
    all_to_all x1, starting transfers between devices, body(): lax.all_to_all(orbitals.reshape(SIDE * SIDE, NG, NG), ('zh', 'y'), 0, 0,...  18.1 us
    ppermute x6, waiting for transfers between devices, shift(): lax.ppermute(values, axes, [(i, (i + by) % count) for i in range(count)])  16.2 us
    all_to_all x1, waiting for transfers between devices, body(): lax.all_to_all(jnp.broadcast_to(sent, (SIDE,) + sent.shape), 'zl', 0, 0,...  11.7 us
  transfers between devices with their start and end apart: 9, of which 4 were waited for; matrix products, arithmetic and copies ran while one was open for 1% of the time, Pallas kernels for 0%

profile of v2, /device:TPU:24, one launch (start us, length us, event | category | flops | bytes accessed | tf_op | source)
XLA Modules:
  0.0 247.4 jit_solution(900011652698605529)
XLA Ops:
  0.0 0.0 copy-start
  0.0 0.0 copy-start.8
  0.0 0.0 copy-start.9
  0.0 0.0 copy-start.10
  0.0 18.1 %all-to-all-start = ((f32[16,128,128]{2,1,0:T(8,128)}), f32[16,128,128]{2,1,0:T(8,128)S(1)}, u32[]{:S(2)}, u32[]{:S(2)}) async-start(f32[16,128,128]{2,1,0:T(8,128)} %bitcast.59), calls=%async_computation | async-start | bytes 2097152 | tf_op jit(solution)/shard_map/all_to_all | solution.py:147
  18.1 0.0 copy-done.9
  18.1 0.6 fusion.18
  22.6 0.0 copy-done.8
  22.7 2.1 collective-permute-start
  24.7 0.0 copy-start.6
  24.7 0.0 copy-start.7
  24.8 4.8 %collective-permute-start.1 = (f32[2,128,128]{2,1,0:T(8,128)S(1)}, f32[2,128,128]{2,1,0:T(8,128)S(1)}, u32[]{:S(2)}, u32[]{:S(2)}) collective-permute-start(f32[2,128,128]{2,1,0:T(8,128)S(1)} %pad_maximum_fusion.1), channel_id=1, source_target_pairs={{0,256},{128,384},{256,0},{384,128},{1,257},{129,385},{257,1},{385... | collective-permute-start | bytes 393224 | tf_op jit(solution)/shard_map/ppermute | solution.py:139
  29.6 1.9 collective-permute-start.2
  31.6 0.0 copy-done.10
  31.6 0.7 fusion.16
  35.9 0.0 collective-permute-done
  35.9 0.0 collective-permute-done.1
  35.9 2.5 %collective-permute-done.2 = f32[2,128,128]{2,1,0:T(8,128)} collective-permute-done((f32[2,128,128]{2,1,0:T(8,128)S(1)}, f32[2,128,128]{2,1,0:T(8,128)}, u32[]{:S(2)}, u32[]{:S(2)}) %collective-permute-start.2) | collective-permute-done | bytes 131104 | tf_op jit(solution)/shard_map/ppermute | solution.py:139
  38.4 0.9 fusion
  39.4 2.3 collective-permute-start.3
  41.7 4.6 %collective-permute-start.4 = (f32[2,32,128]{2,1,0:T(8,128)S(1)}, f32[2,32,128]{2,1,0:T(8,128)S(1)}, u32[]{:S(2)}, u32[]{:S(2)}) collective-permute-start(f32[2,32,128]{2,1,0:T(8,128)S(1)} %get-tuple-element.27), channel_id=1, source_target_pairs={{0,64},{32,96},{64,0},{96,32},{1,65},{33,97},{65,1},{97,33},{2,66}... | collective-permute-start | bytes 98312 | tf_op jit(solution)/shard_map/ppermute | solution.py:139
  46.3 2.7 %collective-permute-start.5 = (f32[2,32,128]{2,1,0:T(8,128)S(1)}, f32[2,32,128]{2,1,0:T(8,128)S(1)}, u32[]{:S(2)}, u32[]{:S(2)}) collective-permute-start(f32[2,32,128]{2,1,0:T(8,128)S(1)} %get-tuple-element.28), channel_id=1, source_target_pairs={{0,96},{32,0},{64,32},{96,64},{1,97},{33,1},{65,33},{97,65},{2,98}... | collective-permute-start | bytes 98312 | tf_op jit(solution)/shard_map/ppermute | solution.py:139
  52.9 0.0 collective-permute-done.3
  52.9 0.0 collective-permute-done.4
  52.9 13.6 %collective-permute-done.5 = f32[2,32,128]{2,1,0:T(8,128)S(1)} collective-permute-done((f32[2,32,128]{2,1,0:T(8,128)S(1)}, f32[2,32,128]{2,1,0:T(8,128)S(1)}, u32[]{:S(2)}, u32[]{:S(2)}) %collective-permute-start.5) | collective-permute-done | bytes 32800 | tf_op jit(solution)/shard_map/ppermute | solution.py:139
  66.6 0.0 all-to-all-done.psi_ref
  66.6 26.1 %all_to_all.30 = f32[4,2,32,128]{3,2,1,0:T(8,128)S(1)} all-to-all(f32[4,2,32,128]{3,2,1,0:T(8,128)S(1)} %broadcast_in_dim.6), channel_id=1, replica_groups=mesh['y'=4,'zl'=4,'zh'=4,'x'=4,'c'=2] {'zh'}, dimensions={0} | all-to-all | bytes 262144 | tf_op jit(solution)/shard_map/all_to_all | solution.py:164
  92.7 0.9 broadcast_in_dim.7
  93.5 3.5 %all-to-all-start.2 = ((f32[4,4,2,32,128]{4,3,2,1,0:T(8,128)}), f32[4,4,2,32,128]{4,3,2,1,0:T(8,128)S(1)}, u32[]{:S(2)}, u32[]{:S(2)}) async-start(f32[4,4,2,32,128]{4,3,2,1,0:T(8,128)} %broadcast_in_dim.7), calls=%async_computation.2 | async-start | bytes 1048576 | tf_op jit(solution)/shard_map/all_to_all | solution.py:165
  97.0 0.1 pad_add_fusion.place_ref
  97.1 0.0 copy-done
  97.1 0.1 constant_dynamic-slice_fusion
  97.2 11.7 %all-to-all-done.2 = f32[4,4,2,32,128]{4,3,2,1,0:T(8,128)S(1)} async-done(((f32[4,4,2,32,128]{4,3,2,1,0:T(8,128)}), f32[4,4,2,32,128]{4,3,2,1,0:T(8,128)S(1)}, u32[]{:S(2)}, u32[]{:S(2)}) %all-to-all-start.2) | async-done | bytes 524320 | tf_op jit(solution)/shard_map/all_to_all | solution.py:165
  108.9 0.0 copy-done.6
  108.9 0.0 copy-done.7
  108.9 2.8 %shard_map.100 = f32[32,16,8,128]{3,2,1,0:T(8,128)S(1)} custom-call(s32[20]{0:T(128)S(1)} %pad_add_fusion.place_ref, f32[16,128,128]{2,1,0:T(8,128)S(1)} %all-to-all-done.psi_ref, f32[16,2,32,128]{3,2,1,0:T(8,128)S(1)} %bitcast.55, bf16[2,256,256]{2,1,0:T(8,128)(2,1)S(1)} %copy-done.6, bf16[2,256,256]{2,1,0:T(8,128)(2,1)S(1)} %copy-done.7), custom_call_target="tpu_custom_call" | custom-call | flops 1610612736 | bytes 4194304 | tf_op jit(solution)/shard_map/pallas_call | solution.py:128
  111.7 0.0 copy-start.1
  111.7 1.3 copy-done.1
  113.0 0.0 copy-start.4
  113.0 7.8 %all-to-all-start.3 = ((f32[32,16,8,128]{3,2,1,0:T(8,128)}), f32[32,16,8,128]{3,2,1,0:T(8,128)S(1)}, u32[]{:S(2)}, u32[]{:S(2)}) async-start(f32[32,16,8,128]{3,2,1,0:T(8,128)} %copy-done.1), calls=%async_computation.3 | async-start | bytes 4194304 | tf_op jit(solution)/shard_map/all_to_all | solution.py:177
  120.8 18.6 %all-gather = f32[512,128]{1,0:T(8,128)S(1)} all-gather(f32[128,128]{1,0:T(8,128)S(1)} %bitcast.60), channel_id=2, replica_groups=mesh['y'=4,'zl'=4,'zh'=4,'x'=4,'c'=2] {'zh'}, dimensions={0}, use_global_device_ids=true | all-gather | bytes 327680 | tf_op jit(solution)/shard_map/all_gather | solution.py:173
  139.4 8.6 %all-to-all-done.3 = f32[32,16,8,128]{3,2,1,0:T(8,128)S(1)} async-done(((f32[32,16,8,128]{3,2,1,0:T(8,128)}), f32[32,16,8,128]{3,2,1,0:T(8,128)S(1)}, u32[]{:S(2)}, u32[]{:S(2)}) %all-to-all-start.3) | async-done | bytes 2097184 | tf_op jit(solution)/shard_map/all_to_all | solution.py:177
  148.0 0.0 copy-done.4
  148.0 0.0 copy-start.5
  148.0 0.9 copy-done.5
  148.9 4.8 %shard_map.101 = f32[4096,128]{1,0:T(8,128)S(1)} custom-call(s32[20]{0:T(128)S(1)} %pad_add_fusion.place_ref, f32[4096,128]{1,0:T(8,128)S(1)} %bitcast.53, f32[4,128,128]{2,1,0:T(8,128)S(1)} %bitcast.57, bf16[2,256,256]{2,1,0:T(8,128)(2,1)S(1)} %copy-done.4, bf16[2,256,256]{2,1,0:T(8,128)(2,1)S(1)} %copy-done.5), custom_call_target="tpu_custom_call" | custom-call | flops 1610612736 | bytes 4980736 | tf_op jit(solution)/shard_map/pallas_call | solution.py:128
  153.8 0.0 copy-start.2
  153.8 0.0 copy-start.3
  153.8 32.3 %all_to_all.31.in_ref = f32[32,16,8,128]{3,2,1,0:T(8,128)S(1)} all-to-all(f32[32,16,8,128]{3,2,1,0:T(8,128)S(1)} %bitcast.54), channel_id=1, replica_groups=mesh['y'=4,'zl'=4,'zh'=4,'x'=4,'c'=2] {'y','x','c'}, dimensions={0} | all-to-all | bytes 4194304 | tf_op jit(solution)/shard_map/all_to_all | solution.py:179
  186.1 0.0 copy-done.2
  186.1 0.0 copy-done.3
  186.1 2.9 %shard_map.102 = f32[16,128,128]{2,1,0:T(8,128)S(1)} custom-call(s32[20]{0:T(128)S(1)} %pad_add_fusion.place_ref, f32[32,16,8,128]{3,2,1,0:T(8,128)S(1)} %all_to_all.31.in_ref, f32[16,2,32,128]{3,2,1,0:T(8,128)S(1)} %bitcast.56, bf16[2,256,256]{2,1,0:T(8,128)(2,1)S(1)} %copy-done.2, bf16[2,256,256]{2,1,0:T(8,128)(2,1)S(1)} %copy-done.3), custom_call_target="tpu_custom_call" | custom-call | flops 1610612736 | bytes 4194304 | tf_op jit(solution)/shard_map/pallas_call | solution.py:128
  189.0 57.5 %all_to_all.32 = f32[16,128,128]{2,1,0:T(8,128)S(1)} all-to-all(f32[16,128,128]{2,1,0:T(8,128)S(1)} %shard_map.102), channel_id=1, replica_groups=mesh['y'=4,'zl'=4,'zh'=4,'x'=4,'c'=2] {'zh','y'}, dimensions={0} | all-to-all | bytes 2097152 | tf_op jit(solution)/shard_map/all_to_all | solution.py:181
  246.4 1.0 copy.12
  (11 shorter events, 0.2 us)
Async XLA Ops:
  0.0 97.1 %copy-start = (f32[128,4,128]{2,1,0:T(4,128)S(1)}, f32[128,4,128]{2,1,0:T(4,128)}, u32[]{:S(2)}) copy-start(f32[128,4,128]{2,1,0:T(4,128)} %param.11) | copy-start | bytes 786436
  0.0 22.6 %copy-start.8 = (f32[4,4,128,128]{3,2,1,0:T(8,128)S(1)}, f32[4,4,128,128]{3,2,1,0:T(8,128)}, u32[]{:S(2)}) copy-start(f32[4,4,128,128]{3,2,1,0:T(8,128)} %param.10) | copy-start | bytes 3145732
  0.0 18.1 %copy-start.9 = (s32[2,1]{0,1:T(1,128)S(1)}, s32[2,1]{0,1:T(1,128)}, u32[]{:S(2)}) copy-start(s32[2,1]{0,1:T(1,128)} %param.13) | copy-start | bytes 28
  0.0 31.5 %copy-start.10 = (s32[2]{0:T(128)S(1)}, s32[2]{0:T(128)}, u32[]{:S(2)}) copy-start(s32[2]{0:T(128)} %param.12) | copy-start | bytes 28
  0.0 66.6 %all-to-all-start = ((f32[16,128,128]{2,1,0:T(8,128)}), f32[16,128,128]{2,1,0:T(8,128)S(1)}, u32[]{:S(2)}, u32[]{:S(2)}) async-start(f32[16,128,128]{2,1,0:T(8,128)} %bitcast.59), calls=%async_computation | async-start | bytes 2097152 | tf_op jit(solution)/shard_map/all_to_all | solution.py:147
  22.7 13.2 %collective-permute-start = (f32[2,128,128]{2,1,0:T(8,128)S(1)}, f32[2,128,128]{2,1,0:T(8,128)S(1)}, u32[]{:S(2)}, u32[]{:S(2)}) collective-permute-start(f32[2,128,128]{2,1,0:T(8,128)S(1)} %pad_maximum_fusion), channel_id=1, source_target_pairs={{0,128},{128,256},{256,384},{384,0},{1,129},{129,257},{257,385},{3... | collective-permute-start | bytes 393224 | tf_op jit(solution)/shard_map/ppermute | solution.py:139
  24.7 84.1 %copy-start.6 = (bf16[2,256,256]{2,1,0:T(8,128)(2,1)S(1)}, bf16[2,256,256]{2,1,0:T(8,128)(2,1)}, u32[]{:S(2)}) copy-start(bf16[2,256,256]{2,1,0:T(8,128)(2,1)} %constant.148.clone.z_ref) | copy-start | bytes 786436
  24.7 84.1 %copy-start.7 = (bf16[2,256,256]{2,1,0:T(8,128)(2,1)S(1)}, bf16[2,256,256]{2,1,0:T(8,128)(2,1)}, u32[]{:S(2)}) copy-start(bf16[2,256,256]{2,1,0:T(8,128)(2,1)} %constant.149.clone.y_ref) | copy-start | bytes 786436
  24.8 11.1 %collective-permute-start.1 = (f32[2,128,128]{2,1,0:T(8,128)S(1)}, f32[2,128,128]{2,1,0:T(8,128)S(1)}, u32[]{:S(2)}, u32[]{:S(2)}) collective-permute-start(f32[2,128,128]{2,1,0:T(8,128)S(1)} %pad_maximum_fusion.1), channel_id=1, source_target_pairs={{0,256},{128,384},{256,0},{384,128},{1,257},{129,385},{257,1},{385... | collective-permute-start | bytes 393224 | tf_op jit(solution)/shard_map/ppermute | solution.py:139
  29.6 8.8 %collective-permute-start.2 = (f32[2,128,128]{2,1,0:T(8,128)S(1)}, f32[2,128,128]{2,1,0:T(8,128)}, u32[]{:S(2)}, u32[]{:S(2)}) collective-permute-start(f32[2,128,128]{2,1,0:T(8,128)S(1)} %pad_maximum_fusion.2), channel_id=1, source_target_pairs={{0,384},{128,0},{256,128},{384,256},{1,385},{129,1},{257,129},{385... | collective-permute-start | bytes 393224 | tf_op jit(solution)/shard_map/ppermute | solution.py:139
  39.4 13.6 %collective-permute-start.3 = (f32[2,32,128]{2,1,0:T(8,128)S(1)}, f32[2,32,128]{2,1,0:T(8,128)S(1)}, u32[]{:S(2)}, u32[]{:S(2)}) collective-permute-start(f32[2,32,128]{2,1,0:T(8,128)S(1)} %get-tuple-element.26), channel_id=1, source_target_pairs={{0,32},{32,64},{64,96},{96,0},{1,33},{33,65},{65,97},{97,1},{2,34}... | collective-permute-start | bytes 98312 | tf_op jit(solution)/shard_map/ppermute | solution.py:139
  41.7 11.3 %collective-permute-start.4 = (f32[2,32,128]{2,1,0:T(8,128)S(1)}, f32[2,32,128]{2,1,0:T(8,128)S(1)}, u32[]{:S(2)}, u32[]{:S(2)}) collective-permute-start(f32[2,32,128]{2,1,0:T(8,128)S(1)} %get-tuple-element.27), channel_id=1, source_target_pairs={{0,64},{32,96},{64,0},{96,32},{1,65},{33,97},{65,1},{97,33},{2,66}... | collective-permute-start | bytes 98312 | tf_op jit(solution)/shard_map/ppermute | solution.py:139
  46.3 20.3 %collective-permute-start.5 = (f32[2,32,128]{2,1,0:T(8,128)S(1)}, f32[2,32,128]{2,1,0:T(8,128)S(1)}, u32[]{:S(2)}, u32[]{:S(2)}) collective-permute-start(f32[2,32,128]{2,1,0:T(8,128)S(1)} %get-tuple-element.28), channel_id=1, source_target_pairs={{0,96},{32,0},{64,32},{96,64},{1,97},{33,1},{65,33},{97,65},{2,98}... | collective-permute-start | bytes 98312 | tf_op jit(solution)/shard_map/ppermute | solution.py:139
  93.5 15.3 %all-to-all-start.2 = ((f32[4,4,2,32,128]{4,3,2,1,0:T(8,128)}), f32[4,4,2,32,128]{4,3,2,1,0:T(8,128)S(1)}, u32[]{:S(2)}, u32[]{:S(2)}) async-start(f32[4,4,2,32,128]{4,3,2,1,0:T(8,128)} %broadcast_in_dim.7), calls=%async_computation.2 | async-start | bytes 1048576 | tf_op jit(solution)/shard_map/all_to_all | solution.py:165
  111.7 1.3 copy-start.1
  113.0 35.0 %copy-start.4 = (bf16[2,256,256]{2,1,0:T(8,128)(2,1)S(1)}, bf16[2,256,256]{2,1,0:T(8,128)(2,1)}, u32[]{:S(2)}) copy-start(bf16[2,256,256]{2,1,0:T(8,128)(2,1)} %constant.150.clone.fwd_ref) | copy-start | bytes 786436
  113.0 35.0 %all-to-all-start.3 = ((f32[32,16,8,128]{3,2,1,0:T(8,128)}), f32[32,16,8,128]{3,2,1,0:T(8,128)S(1)}, u32[]{:S(2)}, u32[]{:S(2)}) async-start(f32[32,16,8,128]{3,2,1,0:T(8,128)} %copy-done.1), calls=%async_computation.3 | async-start | bytes 4194304 | tf_op jit(solution)/shard_map/all_to_all | solution.py:177
  148.0 1.0 copy-start.5
  153.8 32.3 %copy-start.2 = (bf16[2,256,256]{2,1,0:T(8,128)(2,1)S(1)}, bf16[2,256,256]{2,1,0:T(8,128)(2,1)}, u32[]{:S(2)}) copy-start(bf16[2,256,256]{2,1,0:T(8,128)(2,1)} %constant.152.clone.y_ref) | copy-start | bytes 786436
  153.8 32.3 %copy-start.3 = (bf16[2,256,256]{2,1,0:T(8,128)(2,1)S(1)}, bf16[2,256,256]{2,1,0:T(8,128)(2,1)}, u32[]{:S(2)}) copy-start(bf16[2,256,256]{2,1,0:T(8,128)(2,1)} %constant.153.clone.z_ref) | copy-start | bytes 786436

commit v3 on v2

--- a/solution.py
+++ b/solution.py
@@ -61,13 +61,13 @@
     return dot(table[0], high) + (dot(table[0], low) + dot(table[1], high))
 
 
-def plane(sent_ref, place_ref, b, s):
-    return jnp.concatenate([sent_ref[place_ref[b * SIDE + q], s] for q in range(SIDE)], axis=0)
+def plane(sent_ref, b, s):
+    return jnp.concatenate([sent_ref[q * SIDE + b, s] for q in range(SIDE)], axis=0)
 
 
-def forward_kernel(place_ref, psi_ref, sent_ref, z_ref, y_ref, out_ref):
+def forward_kernel(psi_ref, sent_ref, z_ref, y_ref, out_ref):
     for b in range(SIDE):
-        first, second = plane(sent_ref, place_ref, b, 0), plane(sent_ref, place_ref, b, 1)
+        first, second = plane(sent_ref, b, 0), plane(sent_ref, b, 1)
         rows = []
         for a in range(SIDE):
             psi = psi_ref[b * SIDE + a]
@@ -82,7 +82,7 @@
             out_ref[:, b * SIDE + a] = spectrum[:, a * NG : (a + 1) * NG].reshape(GROUP, 8, NG)
 
 
-def middle_kernel(place_ref, in_ref, kernel_ref, fwd_ref, inv_ref, out_ref):
+def middle_kernel(in_ref, kernel_ref, fwd_ref, inv_ref, out_ref):
     for ky in range(SIDE):
         cols = []
         for a in range(SIDE):
@@ -91,7 +91,7 @@
                 jnp.concatenate([in_ref[pl.ds(at, NG, stride=32), :], in_ref[pl.ds(at + 4, NG, stride=32), :]], axis=0)
             )
         spectrum = apply(fwd_ref, jnp.concatenate(cols, axis=1))
-        weight = kernel_ref[place_ref[16 + ky]]
+        weight = kernel_ref[ky]
         weight = jnp.concatenate([weight, weight], axis=0)
         weight = jnp.concatenate([weight] * SIDE, axis=1)
         back = apply(inv_ref, spectrum * weight)
@@ -102,9 +102,9 @@
             out_ref[pl.ds(at + 4, NG, stride=32), :] = part[NG:]
 
 
-def inverse_kernel(place_ref, in_ref, sent_ref, y_ref, z_ref, out_ref):
+def inverse_kernel(in_ref, sent_ref, y_ref, z_ref, out_ref):
     for b in range(SIDE):
-        first, second = plane(sent_ref, place_ref, b, 0), plane(sent_ref, place_ref, b, 1)
+        first, second = plane(sent_ref, b, 0), plane(sent_ref, b, 1)
         cols = [in_ref[:, b * SIDE + a].reshape(2 * NG, NG) for a in range(SIDE)]
         lines = apply(y_ref, jnp.concatenate(cols, axis=1))
         rows = []
@@ -120,7 +120,7 @@
 WORK = 2 * 2 * 3 * 2048 * 256 * 256
 
 
-def call(kernel, shapes, place, *args):
+def call(kernel, shapes, *args):
     moved = sum(int(np.prod(a.shape)) * a.dtype.itemsize for a in args)
     moved += 4 * sum(int(np.prod(shape)) for shape in shapes)
     shapes = [jax.ShapeDtypeStruct(shape, jnp.float32) for shape in shapes]
@@ -128,11 +128,11 @@
     return pl.pallas_call(
         kernel,
         out_shape=shapes,
-        in_specs=[pl.BlockSpec(memory_space=pltpu.SMEM)] + [whole] * len(args),
+        in_specs=[whole] * len(args),
         out_specs=[whole] * len(shapes),
         compiler_params=pltpu.CompilerParams(vmem_limit_bytes=40 * 1024 * 1024),
         cost_estimate=pl.CostEstimate(flops=WORK, bytes_accessed=moved, transcendentals=0),
-    )(place, *args)
+    )(*args)
 
 
 def shift(values, axes, count, by):
@@ -164,20 +164,17 @@
     sent = lax.all_to_all(jnp.broadcast_to(sent, (SIDE,) + sent.shape), "zh", 0, 0, tiled=True)
     sent = lax.all_to_all(jnp.broadcast_to(sent, (SIDE,) + sent.shape), "zl", 0, 0, tiled=True)
     sent = sent.reshape(16, steps, 32, NG)
-    place = jnp.arange(16, dtype=jnp.int32)
-    quarter = place % SIDE * SIDE + place // SIDE
-    place = jnp.concatenate([quarter, jnp.arange(SIDE, dtype=jnp.int32)])
 
     own = lax.dynamic_index_in_dim(kernel, y, 1, keepdims=False)
     own, psi, sent = lax.optimization_barrier((own, psi, sent))
     weight = lax.all_gather(own, "zh", axis=0, tiled=False)
 
     group = ("y", "x", "c")
-    (spectrum,) = call(forward_kernel, [(GROUP, 16, 8, NG)], place, psi, sent, z_fwd, y_fwd)
+    (spectrum,) = call(forward_kernel, [(GROUP, 16, 8, NG)], psi, sent, z_fwd, y_fwd)
     spectrum = lax.all_to_all(spectrum, group, 0, 0, tiled=True).reshape(GROUP * NG, NG)
-    (spectrum,) = call(middle_kernel, [(GROUP * NG, NG)], place, spectrum, weight, x_fwd, x_inv)
+    (spectrum,) = call(middle_kernel, [(GROUP * NG, NG)], spectrum, weight, x_fwd, x_inv)
     spectrum = lax.all_to_all(spectrum.reshape(GROUP, 16, 8, NG), group, 0, 0, tiled=True)
-    (action,) = call(inverse_kernel, [(16, NG, NG)], place, spectrum, sent, y_inv, z_inv)
+    (action,) = call(inverse_kernel, [(16, NG, NG)], spectrum, sent, y_inv, z_inv)
     action = lax.all_to_all(action, ("zh", "y"), 0, 0, tiled=True)
     return action.reshape(SIDE, SIDE, NG, NG)
 

time: 250 us -> 248 us (level)
  no operation moved by 1% of the time
where the time goes in v3:
time: 248 us; the launch traced here: 246 us
  blocking collectives  134 us (54%)
  starting transfers between devices  47.7 us (19%)
  waiting for transfers between devices  36.5 us (15%)
  between operations  11.8 us (5%)
  Pallas kernels  8.77 us (4%)
  local copies, waits for them, and re-layouts  5.53 us (2%)
    all_to_all x1, blocking collectives, body(): action = lax.all_to_all(action, ('zh', 'y'), 0, 0, tiled=True)  57.5 us
    all_to_all x1, blocking collectives, body(): lax.all_to_all(spectrum.reshape(GROUP, 16, 8, NG), group, 0, 0, tiled=True)  32.3 us
    all_to_all x1, blocking collectives, body(): lax.all_to_all(jnp.broadcast_to(sent, (SIDE,) + sent.shape), 'zh', 0, 0,...  26.1 us
    all_gather x1, blocking collectives, body(): weight = lax.all_gather(own, 'zh', axis=0, tiled=False)  18.6 us
    ppermute x6, starting transfers between devices, shift(): lax.ppermute(values, axes, [(i, (i + by) % count) for i in range(count)])  18.4 us
    all_to_all x1, starting transfers between devices, body(): lax.all_to_all(orbitals.reshape(SIDE * SIDE, NG, NG), ('zh', 'y'), 0, 0,...  18.1 us
    ppermute x6, waiting for transfers between devices, shift(): lax.ppermute(values, axes, [(i, (i + by) % count) for i in range(count)])  16.2 us
    all_to_all x1, waiting for transfers between devices, body(): lax.all_to_all(jnp.broadcast_to(sent, (SIDE,) + sent.shape), 'zl', 0, 0,...  11.8 us
  transfers between devices with their start and end apart: 9, of which 4 were waited for; matrix products, arithmetic and copies ran while one was open for 1% of the time, Pallas kernels for 0%

profile of v3, /device:TPU:24, one launch (start us, length us, event | category | flops | bytes accessed | tf_op | source)
XLA Modules:
  0.0 245.8 jit_solution(2791273293193005246)
XLA Ops:
  0.0 0.0 copy-start
  0.0 0.0 copy-start.8
  0.0 0.0 copy-start.9
  0.0 0.0 copy-start.10
  0.0 18.1 %all-to-all-start = ((f32[16,128,128]{2,1,0:T(8,128)}), f32[16,128,128]{2,1,0:T(8,128)S(1)}, u32[]{:S(2)}, u32[]{:S(2)}) async-start(f32[16,128,128]{2,1,0:T(8,128)} %bitcast.59), calls=%async_computation | async-start | bytes 2097152 | tf_op jit(solution)/shard_map/all_to_all | solution.py:147
  18.1 0.0 copy-done.9
  18.1 0.6 fusion.16
  22.6 0.0 copy-done.8
  22.7 0.0 copy-start.6
  22.7 0.0 copy-start.7
  22.7 2.2 collective-permute-start
  24.9 4.7 %collective-permute-start.1 = (f32[2,128,128]{2,1,0:T(8,128)S(1)}, f32[2,128,128]{2,1,0:T(8,128)S(1)}, u32[]{:S(2)}, u32[]{:S(2)}) collective-permute-start(f32[2,128,128]{2,1,0:T(8,128)S(1)} %pad_maximum_fusion.1), channel_id=1, source_target_pairs={{0,256},{128,384},{256,0},{384,128},{1,257},{129,385},{257,1},{385... | collective-permute-start | bytes 393224 | tf_op jit(solution)/shard_map/ppermute | solution.py:139
  29.6 1.9 collective-permute-start.2
  31.6 0.0 copy-done.10
  31.6 0.7 fusion.14
  35.9 0.0 collective-permute-done
  35.9 0.0 collective-permute-done.1
  35.9 2.5 %collective-permute-done.2 = f32[2,128,128]{2,1,0:T(8,128)} collective-permute-done((f32[2,128,128]{2,1,0:T(8,128)S(1)}, f32[2,128,128]{2,1,0:T(8,128)}, u32[]{:S(2)}, u32[]{:S(2)}) %collective-permute-start.2) | collective-permute-done | bytes 131104 | tf_op jit(solution)/shard_map/ppermute | solution.py:139
  38.4 0.9 fusion
  39.4 2.3 collective-permute-start.3
  41.7 4.6 %collective-permute-start.4 = (f32[2,32,128]{2,1,0:T(8,128)S(1)}, f32[2,32,128]{2,1,0:T(8,128)S(1)}, u32[]{:S(2)}, u32[]{:S(2)}) collective-permute-start(f32[2,32,128]{2,1,0:T(8,128)S(1)} %get-tuple-element.27), channel_id=1, source_target_pairs={{0,64},{32,96},{64,0},{96,32},{1,65},{33,97},{65,1},{97,33},{2,66}... | collective-permute-start | bytes 98312 | tf_op jit(solution)/shard_map/ppermute | solution.py:139
  46.3 2.7 %collective-permute-start.5 = (f32[2,32,128]{2,1,0:T(8,128)S(1)}, f32[2,32,128]{2,1,0:T(8,128)S(1)}, u32[]{:S(2)}, u32[]{:S(2)}) collective-permute-start(f32[2,32,128]{2,1,0:T(8,128)S(1)} %get-tuple-element.28), channel_id=1, source_target_pairs={{0,96},{32,0},{64,32},{96,64},{1,97},{33,1},{65,33},{97,65},{2,98}... | collective-permute-start | bytes 98312 | tf_op jit(solution)/shard_map/ppermute | solution.py:139
  52.9 0.0 collective-permute-done.3
  52.9 0.0 collective-permute-done.4
  52.9 13.6 %collective-permute-done.5 = f32[2,32,128]{2,1,0:T(8,128)S(1)} collective-permute-done((f32[2,32,128]{2,1,0:T(8,128)S(1)}, f32[2,32,128]{2,1,0:T(8,128)S(1)}, u32[]{:S(2)}, u32[]{:S(2)}) %collective-permute-start.5) | collective-permute-done | bytes 32800 | tf_op jit(solution)/shard_map/ppermute | solution.py:139
  66.6 0.0 all-to-all-done.psi_ref
  66.6 26.1 %all_to_all.30 = f32[4,2,32,128]{3,2,1,0:T(8,128)S(1)} all-to-all(f32[4,2,32,128]{3,2,1,0:T(8,128)S(1)} %broadcast_in_dim.6), channel_id=1, replica_groups=mesh['y'=4,'zl'=4,'zh'=4,'x'=4,'c'=2] {'zh'}, dimensions={0} | all-to-all | bytes 262144 | tf_op jit(solution)/shard_map/all_to_all | solution.py:164
  92.7 0.9 broadcast_in_dim.7
  93.5 3.5 %all-to-all-start.2 = ((f32[4,4,2,32,128]{4,3,2,1,0:T(8,128)}), f32[4,4,2,32,128]{4,3,2,1,0:T(8,128)S(1)}, u32[]{:S(2)}, u32[]{:S(2)}) async-start(f32[4,4,2,32,128]{4,3,2,1,0:T(8,128)} %broadcast_in_dim.7), calls=%async_computation.2 | async-start | bytes 1048576 | tf_op jit(solution)/shard_map/all_to_all | solution.py:165
  97.0 0.0 copy-done
  97.0 0.1 constant_dynamic-slice_fusion
  97.1 11.8 %all-to-all-done.2 = f32[4,4,2,32,128]{4,3,2,1,0:T(8,128)S(1)} async-done(((f32[4,4,2,32,128]{4,3,2,1,0:T(8,128)}), f32[4,4,2,32,128]{4,3,2,1,0:T(8,128)S(1)}, u32[]{:S(2)}, u32[]{:S(2)}) %all-to-all-start.2) | async-done | bytes 524320 | tf_op jit(solution)/shard_map/all_to_all | solution.py:165
  108.9 0.0 copy-done.6
  108.9 0.0 copy-done.7
  108.9 2.2 shard_map.100
  111.1 0.0 copy-start.1
  111.1 1.3 copy-done.1
  112.5 0.0 copy-start.4
  112.5 7.8 %all-to-all-start.3 = ((f32[32,16,8,128]{3,2,1,0:T(8,128)}), f32[32,16,8,128]{3,2,1,0:T(8,128)S(1)}, u32[]{:S(2)}, u32[]{:S(2)}) async-start(f32[32,16,8,128]{3,2,1,0:T(8,128)} %copy-done.1), calls=%async_computation.3 | async-start | bytes 4194304 | tf_op jit(solution)/shard_map/all_to_all | solution.py:174
  120.2 18.6 %all-gather = f32[512,128]{1,0:T(8,128)S(1)} all-gather(f32[128,128]{1,0:T(8,128)S(1)} %bitcast.60), channel_id=2, replica_groups=mesh['y'=4,'zl'=4,'zh'=4,'x'=4,'c'=2] {'zh'}, dimensions={0}, use_global_device_ids=true | all-gather | bytes 327680 | tf_op jit(solution)/shard_map/all_gather | solution.py:170
  138.8 8.6 %all-to-all-done.3 = f32[32,16,8,128]{3,2,1,0:T(8,128)S(1)} async-done(((f32[32,16,8,128]{3,2,1,0:T(8,128)}), f32[32,16,8,128]{3,2,1,0:T(8,128)S(1)}, u32[]{:S(2)}, u32[]{:S(2)}) %all-to-all-start.3) | async-done | bytes 2097184 | tf_op jit(solution)/shard_map/all_to_all | solution.py:174
  147.5 0.0 copy-done.4
  147.5 0.0 copy-start.5
  147.5 0.9 copy-done.5
  148.4 4.3 %shard_map.101 = f32[4096,128]{1,0:T(8,128)S(1)} custom-call(f32[4096,128]{1,0:T(8,128)S(1)} %bitcast.53, f32[4,128,128]{2,1,0:T(8,128)S(1)} %bitcast.57, bf16[2,256,256]{2,1,0:T(8,128)(2,1)S(1)} %copy-done.4, bf16[2,256,256]{2,1,0:T(8,128)(2,1)S(1)} %copy-done.5), custom_call_target="tpu_custom_call" | custom-call | flops 1610612736 | bytes 4980736 | tf_op jit(solution)/shard_map/pallas_call | solution.py:128
  152.7 0.0 copy-start.2
  152.7 0.0 copy-start.3
  152.7 32.3 %all_to_all.31.in_ref = f32[32,16,8,128]{3,2,1,0:T(8,128)S(1)} all-to-all(f32[32,16,8,128]{3,2,1,0:T(8,128)S(1)} %bitcast.54), channel_id=1, replica_groups=mesh['y'=4,'zl'=4,'zh'=4,'x'=4,'c'=2] {'y','x','c'}, dimensions={0} | all-to-all | bytes 4194304 | tf_op jit(solution)/shard_map/all_to_all | solution.py:176
  185.0 0.0 copy-done.2
  185.0 0.0 copy-done.3
  185.0 2.3 shard_map.102
  187.3 57.5 %all_to_all.32 = f32[16,128,128]{2,1,0:T(8,128)S(1)} all-to-all(f32[16,128,128]{2,1,0:T(8,128)S(1)} %shard_map.102), channel_id=1, replica_groups=mesh['y'=4,'zl'=4,'zh'=4,'x'=4,'c'=2] {'zh','y'}, dimensions={0} | all-to-all | bytes 2097152 | tf_op jit(solution)/shard_map/all_to_all | solution.py:178
  244.8 1.0 copy.12
  (9 shorter events, 0.1 us)
Async XLA Ops:
  0.0 97.0 %copy-start = (f32[128,4,128]{2,1,0:T(4,128)S(1)}, f32[128,4,128]{2,1,0:T(4,128)}, u32[]{:S(2)}) copy-start(f32[128,4,128]{2,1,0:T(4,128)} %param.11) | copy-start | bytes 786436
  0.0 22.6 %copy-start.8 = (f32[4,4,128,128]{3,2,1,0:T(8,128)S(1)}, f32[4,4,128,128]{3,2,1,0:T(8,128)}, u32[]{:S(2)}) copy-start(f32[4,4,128,128]{3,2,1,0:T(8,128)} %param.10) | copy-start | bytes 3145732
  0.0 18.1 %copy-start.9 = (s32[2,1]{0,1:T(1,128)S(1)}, s32[2,1]{0,1:T(1,128)}, u32[]{:S(2)}) copy-start(s32[2,1]{0,1:T(1,128)} %param.13) | copy-start | bytes 28
  0.0 31.5 %copy-start.10 = (s32[2]{0:T(128)S(1)}, s32[2]{0:T(128)}, u32[]{:S(2)}) copy-start(s32[2]{0:T(128)} %param.12) | copy-start | bytes 28
  0.0 66.6 %all-to-all-start = ((f32[16,128,128]{2,1,0:T(8,128)}), f32[16,128,128]{2,1,0:T(8,128)S(1)}, u32[]{:S(2)}, u32[]{:S(2)}) async-start(f32[16,128,128]{2,1,0:T(8,128)} %bitcast.59), calls=%async_computation | async-start | bytes 2097152 | tf_op jit(solution)/shard_map/all_to_all | solution.py:147
  22.7 86.2 %copy-start.6 = (bf16[2,256,256]{2,1,0:T(8,128)(2,1)S(1)}, bf16[2,256,256]{2,1,0:T(8,128)(2,1)}, u32[]{:S(2)}) copy-start(bf16[2,256,256]{2,1,0:T(8,128)(2,1)} %constant.127.clone.z_ref) | copy-start | bytes 786436
  22.7 86.2 %copy-start.7 = (bf16[2,256,256]{2,1,0:T(8,128)(2,1)S(1)}, bf16[2,256,256]{2,1,0:T(8,128)(2,1)}, u32[]{:S(2)}) copy-start(bf16[2,256,256]{2,1,0:T(8,128)(2,1)} %constant.128.clone.y_ref) | copy-start | bytes 786436
  22.7 13.2 %collective-permute-start = (f32[2,128,128]{2,1,0:T(8,128)S(1)}, f32[2,128,128]{2,1,0:T(8,128)S(1)}, u32[]{:S(2)}, u32[]{:S(2)}) collective-permute-start(f32[2,128,128]{2,1,0:T(8,128)S(1)} %pad_maximum_fusion), channel_id=1, source_target_pairs={{0,128},{128,256},{256,384},{384,0},{1,129},{129,257},{257,385},{3... | collective-permute-start | bytes 393224 | tf_op jit(solution)/shard_map/ppermute | solution.py:139
  24.9 11.0 %collective-permute-start.1 = (f32[2,128,128]{2,1,0:T(8,128)S(1)}, f32[2,128,128]{2,1,0:T(8,128)S(1)}, u32[]{:S(2)}, u32[]{:S(2)}) collective-permute-start(f32[2,128,128]{2,1,0:T(8,128)S(1)} %pad_maximum_fusion.1), channel_id=1, source_target_pairs={{0,256},{128,384},{256,0},{384,128},{1,257},{129,385},{257,1},{385... | collective-permute-start | bytes 393224 | tf_op jit(solution)/shard_map/ppermute | solution.py:139
  29.6 8.8 %collective-permute-start.2 = (f32[2,128,128]{2,1,0:T(8,128)S(1)}, f32[2,128,128]{2,1,0:T(8,128)}, u32[]{:S(2)}, u32[]{:S(2)}) collective-permute-start(f32[2,128,128]{2,1,0:T(8,128)S(1)} %pad_maximum_fusion.2), channel_id=1, source_target_pairs={{0,384},{128,0},{256,128},{384,256},{1,385},{129,1},{257,129},{385... | collective-permute-start | bytes 393224 | tf_op jit(solution)/shard_map/ppermute | solution.py:139
  39.4 13.6 %collective-permute-start.3 = (f32[2,32,128]{2,1,0:T(8,128)S(1)}, f32[2,32,128]{2,1,0:T(8,128)S(1)}, u32[]{:S(2)}, u32[]{:S(2)}) collective-permute-start(f32[2,32,128]{2,1,0:T(8,128)S(1)} %get-tuple-element.26), channel_id=1, source_target_pairs={{0,32},{32,64},{64,96},{96,0},{1,33},{33,65},{65,97},{97,1},{2,34}... | collective-permute-start | bytes 98312 | tf_op jit(solution)/shard_map/ppermute | solution.py:139
  41.7 11.3 %collective-permute-start.4 = (f32[2,32,128]{2,1,0:T(8,128)S(1)}, f32[2,32,128]{2,1,0:T(8,128)S(1)}, u32[]{:S(2)}, u32[]{:S(2)}) collective-permute-start(f32[2,32,128]{2,1,0:T(8,128)S(1)} %get-tuple-element.27), channel_id=1, source_target_pairs={{0,64},{32,96},{64,0},{96,32},{1,65},{33,97},{65,1},{97,33},{2,66}... | collective-permute-start | bytes 98312 | tf_op jit(solution)/shard_map/ppermute | solution.py:139
  46.3 20.3 %collective-permute-start.5 = (f32[2,32,128]{2,1,0:T(8,128)S(1)}, f32[2,32,128]{2,1,0:T(8,128)S(1)}, u32[]{:S(2)}, u32[]{:S(2)}) collective-permute-start(f32[2,32,128]{2,1,0:T(8,128)S(1)} %get-tuple-element.28), channel_id=1, source_target_pairs={{0,96},{32,0},{64,32},{96,64},{1,97},{33,1},{65,33},{97,65},{2,98}... | collective-permute-start | bytes 98312 | tf_op jit(solution)/shard_map/ppermute | solution.py:139
  93.5 15.3 %all-to-all-start.2 = ((f32[4,4,2,32,128]{4,3,2,1,0:T(8,128)}), f32[4,4,2,32,128]{4,3,2,1,0:T(8,128)S(1)}, u32[]{:S(2)}, u32[]{:S(2)}) async-start(f32[4,4,2,32,128]{4,3,2,1,0:T(8,128)} %broadcast_in_dim.7), calls=%async_computation.2 | async-start | bytes 1048576 | tf_op jit(solution)/shard_map/all_to_all | solution.py:165
  111.1 1.3 copy-start.1
  112.5 35.0 %copy-start.4 = (bf16[2,256,256]{2,1,0:T(8,128)(2,1)S(1)}, bf16[2,256,256]{2,1,0:T(8,128)(2,1)}, u32[]{:S(2)}) copy-start(bf16[2,256,256]{2,1,0:T(8,128)(2,1)} %constant.129.clone.fwd_ref) | copy-start | bytes 786436
  112.5 35.0 %all-to-all-start.3 = ((f32[32,16,8,128]{3,2,1,0:T(8,128)}), f32[32,16,8,128]{3,2,1,0:T(8,128)S(1)}, u32[]{:S(2)}, u32[]{:S(2)}) async-start(f32[32,16,8,128]{3,2,1,0:T(8,128)} %copy-done.1), calls=%async_computation.3 | async-start | bytes 4194304 | tf_op jit(solution)/shard_map/all_to_all | solution.py:174
  147.5 1.0 copy-start.5
  152.7 32.3 %copy-start.2 = (bf16[2,256,256]{2,1,0:T(8,128)(2,1)S(1)}, bf16[2,256,256]{2,1,0:T(8,128)(2,1)}, u32[]{:S(2)}) copy-start(bf16[2,256,256]{2,1,0:T(8,128)(2,1)} %constant.131.clone.y_ref) | copy-start | bytes 786436
  152.7 32.3 %copy-start.3 = (bf16[2,256,256]{2,1,0:T(8,128)(2,1)S(1)}, bf16[2,256,256]{2,1,0:T(8,128)(2,1)}, u32[]{:S(2)}) copy-start(bf16[2,256,256]{2,1,0:T(8,128)(2,1)} %constant.132.clone.z_ref) | copy-start | bytes 786436
